TPU v7x, 512 devices: a whole 4x8x8 slice. The times are simulated.
512 devices in a mesh: dc: 64 (over y, x, core), tp: 8 (over z).
Axes of the slice: x: 4, y: 8, z: 8, core: 2. Of those that a mesh axis runs over, the one named last changes fastest.
Arguments:
- queries: bfloat16 [8192, 8192], P(('dc', 'tp')), may hold values from -10 to 10
- keys: bfloat16 [8192, 1024], P(('dc', 'tp')), may hold values from -4 to 4
- values: bfloat16 [8192, 1024], P(('dc', 'tp')), may hold values from -6 to 6
- document_index: int32 [8192], P('dc'), may hold values from 0 to 15, never falling along the last dimension, each value on 1 to 4096 neighbouring positions
- owner: int32 [8192], P('dc'), may hold values from 0 to 63, as said below
Outputs:
- attended: bfloat16 [8192, 8192], P('dc', 'tp')
Inputs may be any that keep to these rules, and one draw needn't show every extreme that they name: Each owner 0 to 63 is named by exactly 128 rows; of one index's 128 rows at most 4 name the same owner, and in every draw some index sends exactly 4 rows to one owner.
All inputs are finite; a program needn't handle non-finite values.
Results may differ from a plain program's by a relative error of at most 0.0035.
Values may be sent and summed in bfloat16 or wider, within the bound.
A program may use at most 64 MiB of HBM per device.

v0:
```python
import math

import jax
import jax.numpy as jnp
from jax import lax
from jax.sharding import PartitionSpec as P

HEADS = 64
KVH = 8
HEAD_DIM = 128


def pick_block(length):
    for candidate in (512, 256, 128):
        return candidate
    return length


def slot_index(owner, device_count, capacity):
    choose = (owner[:, None] == jnp.arange(device_count, dtype=jnp.int32)[None, :]).astype(
        jnp.int32
    )
    earlier = jnp.cumsum(choose, axis=0) - choose
    ranked = jnp.sum(earlier * choose, axis=1)
    return owner * capacity + ranked


def compact_index(valid, row_count):
    filled = jnp.cumsum(valid.astype(jnp.int32)) - 1
    return jnp.where(valid, filled, row_count)


def per_device(queries, keys, values, document_index, owner):
    device_count = lax.axis_size("dc")
    device_slot = lax.axis_index("dc")
    local_query_rows, local_key_rows, value_local = (
        lax.all_to_all(queries, "tp", split_axis=1, concat_axis=0, tiled=True),
        lax.all_to_all(keys, "tp", split_axis=1, concat_axis=0, tiled=True),
        lax.all_to_all(values, "tp", split_axis=1, concat_axis=0, tiled=True),
    )
    row_count = local_query_rows.shape[0]
    columns = local_query_rows.shape[1]
    kv_local = local_key_rows.shape[1] // HEAD_DIM
    per_group = HEADS // KVH
    capacity = 2 * row_count // device_count
    scaling = 1.0 / math.sqrt(HEAD_DIM)
    places = device_slot * row_count + jnp.arange(row_count, dtype=jnp.int32)
    slots = slot_index(owner, device_count, capacity)
    send_rows = (
        jnp.zeros((device_count * capacity, columns), jnp.bfloat16).at[slots].set(local_query_rows)
    )
    details = (
        jnp.full((device_count * capacity, 2), -1, jnp.int32)
        .at[slots]
        .set(jnp.stack([places, document_index], axis=1))
    )
    got_rows, got_details = (
        lax.all_to_all(send_rows, "dc", split_axis=0, concat_axis=0, tiled=True),
        lax.all_to_all(details, "dc", split_axis=0, concat_axis=0, tiled=True),
    )
    target = compact_index(got_details[:, 0] >= 0, row_count)
    own_rows = jnp.zeros((row_count, columns), jnp.bfloat16).at[target].set(got_rows, mode="drop")
    own_details = jnp.zeros((row_count, 2), jnp.int32).at[target].set(got_details, mode="drop")
    query_place = own_details[:, 0]
    query_doc = own_details[:, 1]
    query_four_heads = own_rows.reshape(row_count, kv_local, per_group, HEAD_DIM)
    initial = (
        jnp.full((kv_local, per_group, row_count), -1e30, jnp.float32),
        jnp.zeros((kv_local, per_group, row_count), jnp.float32),
        jnp.zeros((kv_local, per_group, row_count, HEAD_DIM), jnp.float32),
    )
    running = initial
    key_part = lax.all_gather(local_key_rows, "dc", axis=0, tiled=True)
    value_part = lax.all_gather(value_local, "dc", axis=0, tiled=True)
    doc_part = lax.all_gather(document_index, "dc", axis=0, tiled=True)
    length = key_part.shape[0]
    block = pick_block(length)
    blocks = length // block
    key_tiles = key_part.reshape(blocks, block, kv_local, HEAD_DIM)
    value_tiles = value_part.reshape(blocks, block, kv_local, HEAD_DIM)
    doc_tiles = doc_part.reshape(blocks, block)

    def visit(running, packed):
        key_block_tile, value_tile, doc_tile, number = packed
        key_place = number * block + jnp.arange(block, dtype=jnp.int32)
        allowed = (doc_tile[None, :] == query_doc[:, None]) & (
            key_place[None, :] <= query_place[:, None]
        )

        def running_update(state):
            maxima, totals, weighted = state
            scores = (
                jnp.einsum(
                    "nhwo,yho->hwny",
                    query_four_heads,
                    key_block_tile,
                    preferred_element_type=jnp.float32,
                )
                * scaling
            )
            scores = jnp.where(allowed[None, None], scores, -1e30)
            fresh = jnp.maximum(maxima, jnp.max(scores, axis=-1))
            weights = jnp.where(allowed[None, None], jnp.exp(scores - fresh[..., None]), 0.0)
            shrink = jnp.exp(maxima - fresh)
            totals = totals * shrink + jnp.sum(weights, axis=-1)
            weighted = weighted * shrink[..., None] + jnp.einsum(
                "lvnx,xlh->lvnh",
                weights.astype(jnp.bfloat16),
                value_tile,
                preferred_element_type=jnp.float32,
            )
            return (fresh, totals, weighted)

        running = lax.cond(jnp.any(allowed), running_update, lambda kept: kept, running)
        return (running, None)

    numbers = jnp.arange(blocks, dtype=jnp.int32)
    running, unused = lax.scan(visit, running, (key_tiles, value_tiles, doc_tiles, numbers))
    maxima, totals, weighted = running
    context = weighted / totals[..., None]
    return context.transpose(2, 0, 1, 3).reshape(row_count, columns).astype(jnp.bfloat16)


def solution(mesh):
    return jax.shard_map(
        per_device,
        mesh=mesh,
        in_specs=(
            P(("dc", "tp"), None),
            P(("dc", "tp"), None),
            P(("dc", "tp"), None),
            P("dc"),
            P("dc"),
        ),
        out_specs=P("dc", "tp"),
        check_vma=False,
    )
```

profile of v0, /device:TPU:1, one launch (start us, length us, event | category | flops | bytes accessed | tf_op | source)
XLA Modules:
  0.0 303.0 jit_solution(7809433054404471939)
XLA Ops:
  7.3 17.6 %all_to_all.81 = bf16[16,8,128]{2,0,1:T(8,128)(2,1)} all-to-all(bf16[16,8,128]{2,0,1:T(8,128)(2,1)S(1)} %copy_bitcast_fusion.3), channel_id=1, replica_groups=mesh['dc'=64,'tp'=8] {'tp'}, dimensions={1} | all-to-all | bytes 65536 | tf_op jit(solution)/shard_map/all_to_all | solution.py:38
  25.8 9.9 %all_to_all.82 = bf16[16,8,128]{2,0,1:T(8,128)(2,1)} all-to-all(bf16[16,8,128]{2,0,1:T(8,128)(2,1)S(1)} %copy_bitcast_fusion.2), channel_id=1, replica_groups=mesh['dc'=64,'tp'=8] {'tp'}, dimensions={1} | all-to-all | bytes 65536 | tf_op jit(solution)/shard_map/all_to_all | solution.py:39
  35.7 1.7 copy.70
  37.4 3.5 %all-to-all-start.2 = ((bf16[16,8,1024]{2,0,1:T(8,128)(2,1)}), bf16[16,8,1024]{2,0,1:T(8,128)(2,1)S(1)}, u32[]{:S(2)}, u32[]{:S(2)}) async-start(bf16[16,8,1024]{2,0,1:T(8,128)(2,1)} %bitcast.93), calls=%async_computation.2 | async-start | bytes 524288 | tf_op jit(solution)/shard_map/all_to_all | solution.py:37
  45.1 1.1 copy.47
  46.2 4.1 %all-to-all-done.2 = bf16[16,8,1024]{2,0,1:T(8,128)(2,1)S(1)} async-done(((bf16[16,8,1024]{2,0,1:T(8,128)(2,1)}), bf16[16,8,1024]{2,0,1:T(8,128)(2,1)S(1)}, u32[]{:S(2)}, u32[]{:S(2)}) %all-to-all-start.2) | async-done | bytes 262176 | tf_op jit(solution)/shard_map/all_to_all | solution.py:37
  50.3 14.4 %all-to-all-start = ((s32[64,4,2]{1,2,0:T(2,128)}), s32[64,4,2]{1,2,0:T(2,128)S(1)}, u32[]{:S(2)}, u32[]{:S(2)}) async-start(s32[64,4,2]{1,2,0:T(2,128)} %copy.47), calls=%async_computation | async-start | bytes 131072 | tf_op jit(solution)/shard_map/all_to_all | solution.py:59
  64.7 1.3 scatter_custom_fusion.2
  66.0 1.0 all_to_all.69
  67.0 7.8 %all-to-all-done = s32[64,4,2]{1,2,0:T(2,128)S(1)} async-done(((s32[64,4,2]{1,2,0:T(2,128)}), s32[64,4,2]{1,2,0:T(2,128)S(1)}, u32[]{:S(2)}, u32[]{:S(2)}) %all-to-all-start) | async-done | bytes 2080 | tf_op jit(solution)/shard_map/all_to_all | solution.py:59
  74.8 4.5 %all-to-all-start.3 = ((bf16[64,4,1024]{2,1,0:T(4,128)(2,1)}), bf16[64,4,1024]{2,1,0:T(4,128)(2,1)S(1)}, u32[]{:S(2)}, u32[]{:S(2)}) async-start(bf16[64,4,1024]{2,1,0:T(4,128)(2,1)} %all_to_all.69), calls=%async_computation.3 | async-start | bytes 1048576 | tf_op jit(solution)/shard_map/all_to_all | solution.py:58
  79.3 46.8 %all-gather = s32[64,1,128]{2,1,0:T(1,128)S(1)} all-gather(s32[1,1,128]{2,1,0:T(1,128)S(1)} %bitcast.119), channel_id=1, replica_groups=mesh['dc'=64,'tp'=8] {'dc'}, dimensions={0}, use_global_device_ids=true | all-gather | bytes 33280 | tf_op jit(solution)/shard_map/all_gather | solution.py:75
  128.2 1.2 scatter_custom_fusion.1
  129.8 1.7 scatter_custom_fusion.3
  131.9 59.5 %all-gather.6.cloned.1.call-done = bf16[8192,128]{1,0:T(8,128)(2,1)} async-done(((bf16[128,128]{1,0:T(8,128)(2,1)}), bf16[8192,128]{1,0:T(8,128)(2,1)}) %all-gather.6.cloned.1.call-update) | async-done | bytes 2097168 | tf_op jit(solution)/shard_map/all_gather | solution.py:74
  191.5 103.6 %while.14 = (s32[]{:T(128)}, f32[1,8,128]{2,1,0:T(8,128)S(1)}, f32[1,8,128]{2,1,0:T(8,128)S(1)}, f32[1,8,128,128]{3,2,1,0:T(8,128)S(1)}, s32[16,512]{1,0:T(8,128...) while((s32[]{:T(128)}, f32[1,8,128]{2,1,0:T(8,128)S(1)}, ...), condition=%wide.region_14.15_spmd, body=%wide.region_8.14_spmd.sunk | while | flops 275779072 | bytes 8204571 | solution.py:118
  194.2 3.7 %conditional.2 = ((f32[1,8,128]{2,1,0:T(8,128)S(1)}, f32[1,8,128]{2,1,0:T(8,128)S(1)}, f32[1,8,128,128]{3,2,1,0:T(8,128)S(1)})) conditional(s32[]{:T(128)} %convert_element_type.46, (f32[1,8,128]{2,1,0:T(8,128)S(1)}, f32[1,8,128]{2,1,0:T(8,128)S(1)}, f32[1,8,128,128]{3,2,1,0:T(8,128)S(1)}) %tuple.41, (pred[128,512]{0,1:T(8,128)(4,1)S(1)}, ...), branch_computations={%region_10.10_spmd, %region_11.13_spmd} | conditional | flops 275516416 | bytes 8127520 | solution.py:114
  194.3 1.4 fusion
  195.6 1.7 fusion.3
  200.7 3.7 %conditional.2 = ((f32[1,8,128]{2,1,0:T(8,128)S(1)}, f32[1,8,128]{2,1,0:T(8,128)S(1)}, f32[1,8,128,128]{3,2,1,0:T(8,128)S(1)})) conditional(s32[]{:T(128)} %convert_element_type.46, (f32[1,8,128]{2,1,0:T(8,128)S(1)}, f32[1,8,128]{2,1,0:T(8,128)S(1)}, f32[1,8,128,128]{3,2,1,0:T(8,128)S(1)}) %tuple.41, (pred[128,512]{0,1:T(8,128)(4,1)S(1)}, ...), branch_computations={%region_10.10_spmd, %region_11.13_spmd} | conditional | flops 275516416 | bytes 8127520 | solution.py:114
  200.7 1.4 fusion
  202.1 1.7 fusion.3
  207.2 3.7 %conditional.2 = ((f32[1,8,128]{2,1,0:T(8,128)S(1)}, f32[1,8,128]{2,1,0:T(8,128)S(1)}, f32[1,8,128,128]{3,2,1,0:T(8,128)S(1)})) conditional(s32[]{:T(128)} %convert_element_type.46, (f32[1,8,128]{2,1,0:T(8,128)S(1)}, f32[1,8,128]{2,1,0:T(8,128)S(1)}, f32[1,8,128,128]{3,2,1,0:T(8,128)S(1)}) %tuple.41, (pred[128,512]{0,1:T(8,128)(4,1)S(1)}, ...), branch_computations={%region_10.10_spmd, %region_11.13_spmd} | conditional | flops 275516416 | bytes 8127520 | solution.py:114
  207.2 1.4 fusion
  208.6 1.7 fusion.3
  213.7 3.7 %conditional.2 = ((f32[1,8,128]{2,1,0:T(8,128)S(1)}, f32[1,8,128]{2,1,0:T(8,128)S(1)}, f32[1,8,128,128]{3,2,1,0:T(8,128)S(1)})) conditional(s32[]{:T(128)} %convert_element_type.46, (f32[1,8,128]{2,1,0:T(8,128)S(1)}, f32[1,8,128]{2,1,0:T(8,128)S(1)}, f32[1,8,128,128]{3,2,1,0:T(8,128)S(1)}) %tuple.41, (pred[128,512]{0,1:T(8,128)(4,1)S(1)}, ...), branch_computations={%region_10.10_spmd, %region_11.13_spmd} | conditional | flops 275516416 | bytes 8127520 | solution.py:114
  213.7 1.4 fusion
  215.1 1.7 fusion.3
  220.1 3.7 %conditional.2 = ((f32[1,8,128]{2,1,0:T(8,128)S(1)}, f32[1,8,128]{2,1,0:T(8,128)S(1)}, f32[1,8,128,128]{3,2,1,0:T(8,128)S(1)})) conditional(s32[]{:T(128)} %convert_element_type.46, (f32[1,8,128]{2,1,0:T(8,128)S(1)}, f32[1,8,128]{2,1,0:T(8,128)S(1)}, f32[1,8,128,128]{3,2,1,0:T(8,128)S(1)}) %tuple.41, (pred[128,512]{0,1:T(8,128)(4,1)S(1)}, ...), branch_computations={%region_10.10_spmd, %region_11.13_spmd} | conditional | flops 275516416 | bytes 8127520 | solution.py:114
  220.2 1.4 fusion
  221.5 1.7 fusion.3
  226.6 3.7 %conditional.2 = ((f32[1,8,128]{2,1,0:T(8,128)S(1)}, f32[1,8,128]{2,1,0:T(8,128)S(1)}, f32[1,8,128,128]{3,2,1,0:T(8,128)S(1)})) conditional(s32[]{:T(128)} %convert_element_type.46, (f32[1,8,128]{2,1,0:T(8,128)S(1)}, f32[1,8,128]{2,1,0:T(8,128)S(1)}, f32[1,8,128,128]{3,2,1,0:T(8,128)S(1)}) %tuple.41, (pred[128,512]{0,1:T(8,128)(4,1)S(1)}, ...), branch_computations={%region_10.10_spmd, %region_11.13_spmd} | conditional | flops 275516416 | bytes 8127520 | solution.py:114
  226.6 1.4 fusion
  228.0 1.7 fusion.3
  233.1 3.7 %conditional.2 = ((f32[1,8,128]{2,1,0:T(8,128)S(1)}, f32[1,8,128]{2,1,0:T(8,128)S(1)}, f32[1,8,128,128]{3,2,1,0:T(8,128)S(1)})) conditional(s32[]{:T(128)} %convert_element_type.46, (f32[1,8,128]{2,1,0:T(8,128)S(1)}, f32[1,8,128]{2,1,0:T(8,128)S(1)}, f32[1,8,128,128]{3,2,1,0:T(8,128)S(1)}) %tuple.41, (pred[128,512]{0,1:T(8,128)(4,1)S(1)}, ...), branch_computations={%region_10.10_spmd, %region_11.13_spmd} | conditional | flops 275516416 | bytes 8127520 | solution.py:114
  233.1 1.4 fusion
  234.5 1.7 fusion.3
  239.6 3.7 %conditional.2 = ((f32[1,8,128]{2,1,0:T(8,128)S(1)}, f32[1,8,128]{2,1,0:T(8,128)S(1)}, f32[1,8,128,128]{3,2,1,0:T(8,128)S(1)})) conditional(s32[]{:T(128)} %convert_element_type.46, (f32[1,8,128]{2,1,0:T(8,128)S(1)}, f32[1,8,128]{2,1,0:T(8,128)S(1)}, f32[1,8,128,128]{3,2,1,0:T(8,128)S(1)}) %tuple.41, (pred[128,512]{0,1:T(8,128)(4,1)S(1)}, ...), branch_computations={%region_10.10_spmd, %region_11.13_spmd} | conditional | flops 275516416 | bytes 8127520 | solution.py:114
  239.6 1.4 fusion
  241.0 1.7 fusion.3
  246.0 3.7 %conditional.2 = ((f32[1,8,128]{2,1,0:T(8,128)S(1)}, f32[1,8,128]{2,1,0:T(8,128)S(1)}, f32[1,8,128,128]{3,2,1,0:T(8,128)S(1)})) conditional(s32[]{:T(128)} %convert_element_type.46, (f32[1,8,128]{2,1,0:T(8,128)S(1)}, f32[1,8,128]{2,1,0:T(8,128)S(1)}, f32[1,8,128,128]{3,2,1,0:T(8,128)S(1)}) %tuple.41, (pred[128,512]{0,1:T(8,128)(4,1)S(1)}, ...), branch_computations={%region_10.10_spmd, %region_11.13_spmd} | conditional | flops 275516416 | bytes 8127520 | solution.py:114
  246.0 1.4 fusion
  247.4 1.7 fusion.3
  252.5 3.7 %conditional.2 = ((f32[1,8,128]{2,1,0:T(8,128)S(1)}, f32[1,8,128]{2,1,0:T(8,128)S(1)}, f32[1,8,128,128]{3,2,1,0:T(8,128)S(1)})) conditional(s32[]{:T(128)} %convert_element_type.46, (f32[1,8,128]{2,1,0:T(8,128)S(1)}, f32[1,8,128]{2,1,0:T(8,128)S(1)}, f32[1,8,128,128]{3,2,1,0:T(8,128)S(1)}) %tuple.41, (pred[128,512]{0,1:T(8,128)(4,1)S(1)}, ...), branch_computations={%region_10.10_spmd, %region_11.13_spmd} | conditional | flops 275516416 | bytes 8127520 | solution.py:114
  252.5 1.4 fusion
  253.9 1.7 fusion.3
  259.0 3.7 %conditional.2 = ((f32[1,8,128]{2,1,0:T(8,128)S(1)}, f32[1,8,128]{2,1,0:T(8,128)S(1)}, f32[1,8,128,128]{3,2,1,0:T(8,128)S(1)})) conditional(s32[]{:T(128)} %convert_element_type.46, (f32[1,8,128]{2,1,0:T(8,128)S(1)}, f32[1,8,128]{2,1,0:T(8,128)S(1)}, f32[1,8,128,128]{3,2,1,0:T(8,128)S(1)}) %tuple.41, (pred[128,512]{0,1:T(8,128)(4,1)S(1)}, ...), branch_computations={%region_10.10_spmd, %region_11.13_spmd} | conditional | flops 275516416 | bytes 8127520 | solution.py:114
  259.0 1.4 fusion
  260.4 1.7 fusion.3
  265.4 3.7 %conditional.2 = ((f32[1,8,128]{2,1,0:T(8,128)S(1)}, f32[1,8,128]{2,1,0:T(8,128)S(1)}, f32[1,8,128,128]{3,2,1,0:T(8,128)S(1)})) conditional(s32[]{:T(128)} %convert_element_type.46, (f32[1,8,128]{2,1,0:T(8,128)S(1)}, f32[1,8,128]{2,1,0:T(8,128)S(1)}, f32[1,8,128,128]{3,2,1,0:T(8,128)S(1)}) %tuple.41, (pred[128,512]{0,1:T(8,128)(4,1)S(1)}, ...), branch_computations={%region_10.10_spmd, %region_11.13_spmd} | conditional | flops 275516416 | bytes 8127520 | solution.py:114
  265.5 1.4 fusion
  266.8 1.7 fusion.3
  271.9 3.7 %conditional.2 = ((f32[1,8,128]{2,1,0:T(8,128)S(1)}, f32[1,8,128]{2,1,0:T(8,128)S(1)}, f32[1,8,128,128]{3,2,1,0:T(8,128)S(1)})) conditional(s32[]{:T(128)} %convert_element_type.46, (f32[1,8,128]{2,1,0:T(8,128)S(1)}, f32[1,8,128]{2,1,0:T(8,128)S(1)}, f32[1,8,128,128]{3,2,1,0:T(8,128)S(1)}) %tuple.41, (pred[128,512]{0,1:T(8,128)(4,1)S(1)}, ...), branch_computations={%region_10.10_spmd, %region_11.13_spmd} | conditional | flops 275516416 | bytes 8127520 | solution.py:114
  271.9 1.4 fusion
  273.3 1.7 fusion.3
  278.4 3.7 %conditional.2 = ((f32[1,8,128]{2,1,0:T(8,128)S(1)}, f32[1,8,128]{2,1,0:T(8,128)S(1)}, f32[1,8,128,128]{3,2,1,0:T(8,128)S(1)})) conditional(s32[]{:T(128)} %convert_element_type.46, (f32[1,8,128]{2,1,0:T(8,128)S(1)}, f32[1,8,128]{2,1,0:T(8,128)S(1)}, f32[1,8,128,128]{3,2,1,0:T(8,128)S(1)}) %tuple.41, (pred[128,512]{0,1:T(8,128)(4,1)S(1)}, ...), branch_computations={%region_10.10_spmd, %region_11.13_spmd} | conditional | flops 275516416 | bytes 8127520 | solution.py:114
  278.4 1.4 fusion
  279.8 1.7 fusion.3
  284.9 3.7 %conditional.2 = ((f32[1,8,128]{2,1,0:T(8,128)S(1)}, f32[1,8,128]{2,1,0:T(8,128)S(1)}, f32[1,8,128,128]{3,2,1,0:T(8,128)S(1)})) conditional(s32[]{:T(128)} %convert_element_type.46, (f32[1,8,128]{2,1,0:T(8,128)S(1)}, f32[1,8,128]{2,1,0:T(8,128)S(1)}, f32[1,8,128,128]{3,2,1,0:T(8,128)S(1)}) %tuple.41, (pred[128,512]{0,1:T(8,128)(4,1)S(1)}, ...), branch_computations={%region_10.10_spmd, %region_11.13_spmd} | conditional | flops 275516416 | bytes 8127520 | solution.py:114
  284.9 1.4 fusion
  286.3 1.7 fusion.3
  291.3 3.7 %conditional.2 = ((f32[1,8,128]{2,1,0:T(8,128)S(1)}, f32[1,8,128]{2,1,0:T(8,128)S(1)}, f32[1,8,128,128]{3,2,1,0:T(8,128)S(1)})) conditional(s32[]{:T(128)} %convert_element_type.46, (f32[1,8,128]{2,1,0:T(8,128)S(1)}, f32[1,8,128]{2,1,0:T(8,128)S(1)}, f32[1,8,128,128]{3,2,1,0:T(8,128)S(1)}) %tuple.41, (pred[128,512]{0,1:T(8,128)(4,1)S(1)}, ...), branch_computations={%region_10.10_spmd, %region_11.13_spmd} | conditional | flops 275516416 | bytes 8127520 | solution.py:114
  291.4 1.4 fusion
  292.7 1.7 fusion.3
  (174 shorter events, 41.3 us)
Async XLA Ops:
  6.5 0.8 copy-start
  6.5 125.3 %all-gather.4.cloned.1.call-start = ((), (), s32[]{:S(2)}) async-start(), calls=%async_computation.5 | async-start | bytes 2129920 | tf_op jit(solution)/shard_map/all_gather | solution.py:73
  25.0 166.4 %all-gather.6.cloned.1.call-start = ((), (), s32[]{:S(2)}) async-start(), calls=%async_computation.6 | async-start | bytes 2129920 | tf_op jit(solution)/shard_map/all_gather | solution.py:74
  37.4 41.9 %copy-start.1 = (s32[128]{0:T(128)S(1)}, s32[128]{0:T(128)}, u32[]{:S(2)}) copy-start(s32[128]{0:T(128)} %param.12) | copy-start | bytes 1540
  37.4 12.9 %all-to-all-start.2 = ((bf16[16,8,1024]{2,0,1:T(8,128)(2,1)}), bf16[16,8,1024]{2,0,1:T(8,128)(2,1)S(1)}, u32[]{:S(2)}, u32[]{:S(2)}) async-start(bf16[16,8,1024]{2,0,1:T(8,128)(2,1)} %bitcast.93), calls=%async_computation.2 | async-start | bytes 524288 | tf_op jit(solution)/shard_map/all_to_all | solution.py:37
  50.3 24.5 %all-to-all-start = ((s32[64,4,2]{1,2,0:T(2,128)}), s32[64,4,2]{1,2,0:T(2,128)S(1)}, u32[]{:S(2)}, u32[]{:S(2)}) async-start(s32[64,4,2]{1,2,0:T(2,128)} %copy.47), calls=%async_computation | async-start | bytes 131072 | tf_op jit(solution)/shard_map/all_to_all | solution.py:59
  74.8 54.8 %all-to-all-start.3 = ((bf16[64,4,1024]{2,1,0:T(4,128)(2,1)}), bf16[64,4,1024]{2,1,0:T(4,128)(2,1)S(1)}, u32[]{:S(2)}, u32[]{:S(2)}) async-start(bf16[64,4,1024]{2,1,0:T(4,128)(2,1)} %all_to_all.69), calls=%async_computation.3 | async-start | bytes 1048576 | tf_op jit(solution)/shard_map/all_to_all | solution.py:58
Sparse Core Ops, SparseCore 0:
  25.1 82.5 all-gather.3
  111.1 80.2 all-gather.5
where the time goes:
time: 305 us; the launch traced here: 303 us
  blocking collectives  74.3 us (24%)
  waiting for transfers between devices  71.5 us (23%)
  matrix products  49.6 us (16%)
  other arithmetic  26.4 us (9%)
  local copies, waits for them, and re-layouts  22.8 us (7%)
  starting transfers between devices  22.5 us (7%)
  loops' own time  22.4 us (7%)
  between operations  13.6 us (4%)
    all_gather x1, waiting for transfers between devices, per_device(): value_part = lax.all_gather(value_local, 'dc', axis=0, tiled=True)  59.5 us
    all_gather x1, blocking collectives, per_device(): doc_part = lax.all_gather(document_index, 'dc', axis=0, tiled=True)  46.8 us
    dot_general x16, matrix products, running_update(): jnp.einsum('lvnx,xlh->lvnh', weights.astype(jnp.bfloat16), value_tile, pr...  27.9 us
    dot_general x16, matrix products, running_update(): jnp.einsum('nhwo,yho->hwny', query_four_heads, key_block_tile, preferred_...  21.8 us
    another operation x1, loops' own time, per_device(): lax.scan(visit, running, (key_tiles, value_tiles, doc_tiles, numbers))  21.5 us
    all_to_all x1, blocking collectives, per_device(): lax.all_to_all(keys, 'tp', split_axis=1, concat_axis=0, tiled=True)  17.6 us
    all_to_all x1, starting transfers between devices, per_device(): lax.all_to_all(details, 'dc', split_axis=0, concat_axis=0, tiled=True)  14.4 us
    reduce_or x16, other arithmetic, visit(): jnp.any(allowed)  13.4 us
  transfers between devices with their start and end apart: 5, of which 3 were waited for; matrix products, arithmetic and copies ran while one was open for 5% of the time, Pallas kernels for 0%

commit v1 on v0

v1 whole, which is shorter than its diff:
```python
import math

import jax
import jax.numpy as jnp
from jax import lax
from jax.experimental import pallas as pl
from jax.experimental.pallas import tpu as pltpu
from jax.sharding import PartitionSpec as P

MESH = pl.DeviceIdType.MESH
HEADS = 64
KVH = 8
HEAD_DIM = 128
ROWS = 128
N_DC = 64
N_TP = 8
PER = HEADS // KVH
REACH = 32
SLOTS = 34
PAIR = 2 * ROWS
CAP = 4
GROUP = 4
TILE = CAP * GROUP
DEAD = -1e30
V0, K0, D0, Z0, END = 0, 128, 256, 272, 384
SCALE = math.log2(math.e) / math.sqrt(HEAD_DIM)
F32, BF16, I32 = jnp.float32, jnp.bfloat16, jnp.int32


def iota(shape, dim):
    return lax.broadcasted_iota(I32, shape, dim)


def kernel(
    q_hbm, k_hbm, v_hbm, doc_ref, own_ref, out_ref,
    kin, qin, slots, neg, scores, peak, pack, unpack, context, packed, got, owners,
    kv_send, kv_recv, q_send, q_recv, own_send, own_recv, spread_send, spread_recv, out_send, out_recv,
):
    me = lax.axis_index("dc")
    tp = lax.axis_index("tp")

    barrier = pltpu.get_barrier_semaphore()

    @pl.loop(1, N_TP)
    def _(j):
        pl.semaphore_signal(barrier, inc=1, device_id=(me, lax.rem(tp + j, N_TP)), device_id_type=MESH)

    @pl.loop(1, N_DC)
    def _(j):
        pl.semaphore_signal(barrier, inc=1, device_id=(lax.rem(me + j, N_DC), tp), device_id_type=MESH)

    pl.semaphore_wait(barrier, N_TP - 1 + N_DC - 1)

    mine = pl.ds(pl.multiple_of(tp * 16, 16), 16)

    def columns(t, width):
        return pl.ds(pl.multiple_of(t * width, width), width)

    def part(source, t, width, target, send, recv):
        return pltpu.make_async_remote_copy(
            src_ref=source.at[:, columns(t, width)], dst_ref=target, send_sem=send, recv_sem=recv,
            device_id=(me, t), device_id_type=MESH,
        )

    value_target = slots.at[0, pl.ds(pl.multiple_of(V0 + tp * 16, 16), 16), :]

    @pl.loop(1, N_TP)
    def _(j):
        t = lax.rem(tp + j, N_TP)
        part(k_hbm, t, HEAD_DIM, kin.at[mine, :], kv_send.at[0], kv_recv.at[0]).start()
        part(v_hbm, t, HEAD_DIM, value_target, kv_send.at[1], kv_recv.at[1]).start()

    pltpu.make_async_copy(k_hbm.at[:, columns(tp, HEAD_DIM)], kin.at[mine, :], kv_recv.at[0]).start()
    pltpu.make_async_copy(v_hbm.at[:, columns(tp, HEAD_DIM)], value_target, kv_recv.at[1]).start()

    @pl.loop(1, N_TP)
    def _(j):
        t = lax.rem(tp + j, N_TP)
        part(q_hbm, t, PER * HEAD_DIM, qin.at[mine, :], q_send, q_recv).start()

    pltpu.make_async_copy(q_hbm.at[:, columns(tp, PER * HEAD_DIM)], qin.at[mine, :], q_recv).start()

    @pl.loop(1, N_DC)
    def _(j):
        pltpu.make_async_remote_copy(
            src_ref=own_ref, dst_ref=owners.at[me], send_sem=own_send, recv_sem=own_recv,
            device_id=(lax.rem(me + j, N_DC), tp), device_id_type=MESH,
        ).start()

    pltpu.make_async_copy(own_ref, owners.at[me], own_recv).start()

    slots[:, Z0:END, :] = jnp.zeros((SLOTS, END - Z0, ROWS), BF16)
    reach = jnp.minimum(me, REACH)

    @pl.loop(reach + 1, SLOTS)
    def _(r):
        slots[r, V0:D0, :] = jnp.zeros((D0 - V0, ROWS), BF16)
        slots[r, D0:Z0, :] = jnp.ones((Z0 - D0, ROWS), BF16)

    doc = doc_ref[...]
    slots[0, D0:Z0, :] = jnp.where(iota((Z0 - D0, ROWS), 0) == doc, 1.0, 0.0).astype(BF16)
    other = jnp.where((iota((ROWS, ROWS), 0) != doc) & (iota((ROWS, ROWS), 0) < Z0 - D0), DEAD, 0.0)
    neg[...] = other.T.astype(BF16)

    owner = own_ref[...]
    owner_col = jnp.broadcast_to(owner, (ROWS, ROWS)).astype(F32).T
    same = (owner_col == owner.astype(F32)) & (iota((ROWS, ROWS), 0) < iota((ROWS, ROWS), 1))
    rank = jnp.sum(jnp.where(same, 1.0, 0.0), axis=0, keepdims=True).astype(I32)
    place = owner * TILE + rank
    target = jnp.concatenate([place + h * CAP for h in range(GROUP)], axis=1)

    @pl.loop(0, N_DC * TILE, step=128)
    def _(base):
        base = pl.multiple_of(base, 128)
        rows = iota((128, GROUP * ROWS), 0) + base
        pack[pl.ds(base, 128), :] = jnp.where(rows == target, 1.0, 0.0).astype(BF16)

    pltpu.make_async_copy(kin, kin, kv_recv.at[0]).wait()
    pltpu.make_async_copy(kin, kin, kv_recv.at[1]).wait()
    slots[0, K0:D0, :] = kin[...].astype(F32).T.astype(BF16)

    last = jnp.minimum(N_DC - 1 - me, REACH)

    def spread(r):
        return pltpu.make_async_remote_copy(
            src_ref=slots.at[0, pl.ds(0, Z0), :], dst_ref=slots.at[r, pl.ds(0, Z0), :],
            send_sem=spread_send.at[r], recv_sem=spread_recv.at[r],
            device_id=(me + r, tp), device_id_type=MESH,
        )

    @pl.loop(1, last + 1)
    def _(r):
        spread(r).start()

    pltpu.make_async_copy(owners, owners, own_recv).wait()
    hits = jnp.where(owners[...].reshape(N_DC, ROWS) == me, 1.0, 0.0).astype(BF16)
    counts = lax.dot_general(
        jnp.ones((8, ROWS), BF16), hits, (((1,), (1,)), ((), ())), preferred_element_type=F32
    ).astype(BF16)
    lane_source = iota((N_DC, N_DC * TILE), 1) // TILE
    row_source = iota((N_DC, N_DC * TILE), 0)
    count = jnp.dot(counts, jnp.where(lane_source == row_source, 1.0, 0.0).astype(BF16), preferred_element_type=F32)
    before = jnp.dot(counts, jnp.where(row_source < lane_source, 1.0, 0.0).astype(BF16), preferred_element_type=F32)
    lane = iota((1, N_DC * TILE), 1)
    turn = lane % CAP
    goal = jnp.where(
        turn < count[0:1].astype(I32), before[0:1].astype(I32) + turn + (lane // CAP % GROUP) * ROWS, -1
    )

    @pl.loop(0, GROUP * ROWS, step=64)
    def _(base):
        base = pl.multiple_of(base, 64)
        rows = iota((64, N_DC * TILE), 0) + base
        unpack[pl.ds(base, 64), :] = jnp.where(rows == goal, 1.0, 0.0).astype(BF16)

    pltpu.make_async_copy(qin, qin, q_recv).wait()

    def arrive(r):
        @pl.when((r >= 1) & (r <= reach))
        def _():
            here = slots.at[r, pl.ds(0, Z0), :]
            pltpu.make_async_copy(here, here, spread_recv.at[r]).wait()

    def key_pair(c):
        return jnp.concatenate([slots[2 * c, K0:END, :], slots[2 * c + 1, K0:END, :]], axis=1)

    def score(h, keys):
        queries = jnp.concatenate([qin[:, h * HEAD_DIM : (h + 1) * HEAD_DIM], neg[...]], axis=1)
        return jnp.dot(queries, keys, preferred_element_type=F32)

    arrive(1)
    keys = key_pair(0)
    live = iota((ROWS, PAIR), 1) <= jnp.where(iota((ROWS, PAIR), 1) < ROWS, iota((ROWS, PAIR), 0), PAIR)
    for h in range(PER):
        s = jnp.where(live, score(h, keys), DEAD)
        scores[h, 0] = s
        peak[h] = jnp.maximum(s[:, :ROWS], s[:, ROWS:])

    @pl.loop(1, SLOTS // 2)
    def _(c):
        arrive(2 * c)
        arrive(2 * c + 1)
        keys = key_pair(c)
        for h in range(PER):
            s = score(h, keys)
            scores[h, c] = s
            peak[h] = jnp.maximum(peak[h], jnp.maximum(s[:, :ROWS], s[:, ROWS:]))

    for g in range(PER // GROUP):

        @pl.loop(0, GROUP)
        def _(i):
            h = g * GROUP + i
            top = jnp.broadcast_to(jnp.max(peak[h], axis=1, keepdims=True), (ROWS, PAIR))
            total = jnp.zeros((ROWS, ROWS), F32)
            summed = jnp.zeros((ROWS, HEAD_DIM), F32)
            for c in range(SLOTS // 2):
                weights = jnp.exp2((scores[h, c] - top) * SCALE)
                total = total + (weights[:, :ROWS] + weights[:, ROWS:])
                values = jnp.concatenate([slots[2 * c, V0:K0, :], slots[2 * c + 1, V0:K0, :]], axis=0)
                summed = summed + jnp.dot(weights.astype(BF16), values, preferred_element_type=F32)
            result = summed / jnp.sum(total, axis=1, keepdims=True)
            context[pl.ds(pl.multiple_of(i * ROWS, ROWS), ROWS), :] = result.astype(BF16)

        packed[g] = jnp.dot(pack[...], context[...], preferred_element_type=F32).astype(BF16)

        def tile(r):
            return pl.ds(pl.multiple_of(r * TILE, TILE), TILE)

        @pl.loop(1, N_DC)
        def _(j):
            to = lax.rem(me + j, N_DC)
            pltpu.make_async_remote_copy(
                src_ref=packed.at[g, tile(to), :], dst_ref=got.at[g, tile(me), :],
                send_sem=out_send.at[g], recv_sem=out_recv.at[g], device_id=(to, tp), device_id_type=MESH,
            ).start()

        pltpu.make_async_copy(packed.at[g, tile(me), :], got.at[g, tile(me), :], out_recv.at[g]).start()

    for g in range(PER // GROUP):
        pltpu.make_async_copy(got.at[g], got.at[g], out_recv.at[g]).wait()
        rows = jnp.dot(unpack[...], got[g], preferred_element_type=F32).astype(BF16)
        for i in range(GROUP):
            h = g * GROUP + i
            out_ref[:, h * HEAD_DIM : (h + 1) * HEAD_DIM] = rows[i * ROWS : (i + 1) * ROWS]

    seven = kin.at[pl.ds(0, ROWS - 16), :]
    pltpu.make_async_copy(seven, seven, kv_send.at[0]).wait()
    pltpu.make_async_copy(seven, seven, kv_send.at[1]).wait()
    sent = qin.at[pl.ds(0, ROWS - 16), :]
    pltpu.make_async_copy(sent, sent, q_send).wait()
    sent = owners.at[pl.ds(0, N_DC - 1)]
    pltpu.make_async_copy(sent, sent, own_send).wait()

    @pl.loop(1, last + 1)
    def _(r):
        spread(r).wait_send()

    for g in range(PER // GROUP):
        sent = packed.at[g, pl.ds(0, (N_DC - 1) * TILE), :]
        pltpu.make_async_copy(sent, sent, out_send.at[g]).wait()


def per_device(queries, keys, values, document_index, owner):
    hbm = pl.BlockSpec(memory_space=pl.ANY)
    vmem = pl.BlockSpec(memory_space=pltpu.VMEM)
    dma = pltpu.SemaphoreType.DMA
    groups = PER // GROUP
    return pl.pallas_call(
        kernel,
        out_shape=jax.ShapeDtypeStruct((ROWS, PER * HEAD_DIM), BF16),
        in_specs=[hbm, hbm, hbm, vmem, vmem],
        out_specs=vmem,
        scratch_shapes=[
            pltpu.VMEM((ROWS, HEAD_DIM), BF16),
            pltpu.VMEM((ROWS, PER * HEAD_DIM), BF16),
            pltpu.VMEM((SLOTS, END, ROWS), BF16),
            pltpu.VMEM((ROWS, ROWS), BF16),
            pltpu.VMEM((PER, SLOTS // 2, ROWS, PAIR), F32),
            pltpu.VMEM((PER, ROWS, ROWS), F32),
            pltpu.VMEM((N_DC * TILE, GROUP * ROWS), BF16),
            pltpu.VMEM((GROUP * ROWS, N_DC * TILE), BF16),
            pltpu.VMEM((GROUP * ROWS, HEAD_DIM), BF16),
            pltpu.VMEM((groups, N_DC * TILE, HEAD_DIM), BF16),
            pltpu.VMEM((groups, N_DC * TILE, HEAD_DIM), BF16),
            pltpu.VMEM((N_DC, 1, ROWS), I32),
            dma((2,)), dma((2,)), dma, dma, dma, dma, dma((SLOTS,)), dma((SLOTS,)), dma((groups,)), dma((groups,)),
        ],
        compiler_params=pltpu.CompilerParams(
            collective_id=0, has_side_effects=True, vmem_limit_bytes=48 * 1024 * 1024
        ),
        cost_estimate=pl.CostEstimate(flops=2_300_000_000, bytes_accessed=4_000_000, transcendentals=4_500_000),
    )(queries, keys, values, document_index.reshape(1, ROWS), owner.reshape(1, ROWS))


def solution(mesh):
    return jax.shard_map(
        per_device,
        mesh=mesh,
        in_specs=(
            P(("dc", "tp"), None),
            P(("dc", "tp"), None),
            P(("dc", "tp"), None),
            P("dc"),
            P("dc"),
        ),
        out_specs=P("dc", "tp"),
        check_vma=False,
    )
```

time: 305 us -> 146 us (0.48)
  Pallas kernels: 0 us -> 141 us
  blocking collectives: 74.3 us -> 0 us
  waiting for transfers between devices: 71.5 us -> 0 us
  matrix products: 49.6 us -> 0 us
  other arithmetic: 26.4 us -> 0 us
  starting transfers between devices: 22.5 us -> 0 us
  loops' own time: 22.4 us -> 0 us
  local copies, waits for them, and re-layouts: 22.8 us -> 3.84 us
  between operations: 13.6 us -> 0.01 us
    pallas_call x0 -> x1, Pallas kernels: none -> 141 us  [per_device(): pl.pallas_call(kernel, out_shape=jax.ShapeDtypeStruct((ROWS, PER * HEAD_D...]
    all_gather x2 -> x0, waiting for transfers between devices: 59.6 us -> none  [the longest x1 59.5 us: per_device(): value_part = lax.all_gather(value_local, 'dc', axis=0, tiled=True)]
    dot_general x32 -> x0, matrix products: 49.6 us -> none  [the longest x16 27.9 us: running_update(): jnp.einsum('lvnx,xlh->lvnh', weights.astype(jnp.bfloat16), value_tile, pr...]
    all_gather x1 -> x0, blocking collectives: 46.8 us -> none  [per_device(): doc_part = lax.all_gather(document_index, 'dc', axis=0, tiled=True)]
    all_to_all x2 -> x0, blocking collectives: 27.5 us -> none  [the longest x1 17.6 us: per_device(): lax.all_to_all(keys, 'tp', split_axis=1, concat_axis=0, tiled=True)]
    all_to_all x3 -> x0, starting transfers between devices: 22.4 us -> none  [the longest x1 14.4 us: per_device(): lax.all_to_all(details, 'dc', split_axis=0, concat_axis=0, tiled=True)]
    another operation x17 -> x0, loops' own time: 22.4 us -> none  [the longest x1 21.5 us: per_device(): lax.scan(visit, running, (key_tiles, value_tiles, doc_tiles, numbers))]
    reduce_or x16 -> x0, other arithmetic: 13.4 us -> none  [visit(): jnp.any(allowed)]
  transfers between devices with their start and end apart: 5 -> 0, of which waited for: 3 -> 0; matrix products, arithmetic and copies ran while one was open for 5% -> 0% of each run, Pallas kernels for 0% -> 0%
where the time goes in v1:
time: 146 us; the launch traced here: 145 us
  Pallas kernels  141 us (97%)
  local copies, waits for them, and re-layouts  3.84 us (3%)
    pallas_call x1, Pallas kernels, per_device(): pl.pallas_call(kernel, out_shape=jax.ShapeDtypeStruct((ROWS, PER * HEAD_D...  141 us
    unnamed x11, local copies, waits for them, and re-layouts  3.84 us

profile of v1, /device:TPU:1, one launch (start us, length us, event | category | flops | bytes accessed | tf_op | source)
XLA Modules:
  0.0 145.3 jit_solution(9637408238613577259)
XLA Ops:
  0.0 0.0 copy-start.3
  0.0 0.0 copy-start.4
  0.0 0.7 copy-done.3
  0.7 0.0 copy-done.4
  0.7 0.0 copy-start
  0.7 0.9 copy-done
  1.6 0.0 copy-start.1
  1.6 0.8 copy-done.1
  2.4 0.0 copy-start.2
  2.4 0.8 copy-done.2
  3.1 141.5 %shard_map.55 = bf16[128,1024]{1,0:T(8,128)(2,1)S(1)} custom-call(bf16[16,8192]{1,0:T(8,128)(2,1)S(1)} %copy-done, bf16[16,1024]{1,0:T(8,128)(2,1)S(1)} %copy-done.1, bf16[16,1024]{1,0:T(8,128)(2,1)S(1)} %copy-done.2, s32[1,128]{1,0:T(1,128)S(1)} %bitcast.2, s32[1,128]{1,0:T(1,128)S(1)} %bitcast.3), custom_call_target="tpu_custom_call" | custom-call | flops 2300000000 | bytes 4000000 | tf_op jit(solution)/shard_map/pallas_call | solution.py:249
  144.6 0.7 copy.7
Async XLA Ops:
  0.0 0.7 copy-start.3
  0.0 0.7 copy-start.4
  0.7 0.9 copy-start
  1.6 0.8 copy-start.1
  2.4 0.8 copy-start.2

commit v2 on v1

--- a/solution.py
+++ b/solution.py
@@ -14,6 +14,7 @@
 ROWS = 128
 N_DC = 64
 N_TP = 8
+ROWS_OF_CHIPS, COLS = 8, 4
 PER = HEADS // KVH
 REACH = 32
 SLOTS = 34
@@ -32,13 +33,15 @@
 
 
 def kernel(
-    q_hbm, k_hbm, v_hbm, doc_ref, own_ref, out_ref,
-    kin, qin, slots, neg, scores, peak, pack, unpack, context, packed, got, owners,
-    kv_send, kv_recv, q_send, q_recv, own_send, own_recv, spread_send, spread_recv, out_send, out_recv,
+    q_hbm, k_hbm, v_hbm, doc_hbm, own_hbm, out_ref,
+    kin, qin, slots, neg, scores, peak, pack, unpack, context, packed, got, owners, doc_ref, own_ref,
+    kv_send, kv_recv, q_send, q_recv, own_send, own_recv, doc_sem, down_send, along_send, across_send, spread_recv, out_send, out_recv,
 ):
     me = lax.axis_index("dc")
     tp = lax.axis_index("tp")
 
+    pltpu.make_async_copy(doc_hbm, doc_ref, doc_sem.at[0]).start()
+    pltpu.make_async_copy(own_hbm, own_ref, doc_sem.at[1]).start()
     barrier = pltpu.get_barrier_semaphore()
 
     @pl.loop(1, N_TP)
@@ -80,6 +83,8 @@
 
     pltpu.make_async_copy(q_hbm.at[:, columns(tp, PER * HEAD_DIM)], qin.at[mine, :], q_recv).start()
 
+    pltpu.make_async_copy(own_hbm, own_ref, doc_sem.at[1]).wait()
+
     @pl.loop(1, N_DC)
     def _(j):
         pltpu.make_async_remote_copy(
@@ -97,6 +102,7 @@
         slots[r, V0:D0, :] = jnp.zeros((D0 - V0, ROWS), BF16)
         slots[r, D0:Z0, :] = jnp.ones((Z0 - D0, ROWS), BF16)
 
+    pltpu.make_async_copy(doc_hbm, doc_ref, doc_sem.at[0]).wait()
     doc = doc_ref[...]
     slots[0, D0:Z0, :] = jnp.where(iota((Z0 - D0, ROWS), 0) == doc, 1.0, 0.0).astype(BF16)
     other = jnp.where((iota((ROWS, ROWS), 0) != doc) & (iota((ROWS, ROWS), 0) < Z0 - D0), DEAD, 0.0)
@@ -119,18 +125,61 @@
     pltpu.make_async_copy(kin, kin, kv_recv.at[1]).wait()
     slots[0, K0:D0, :] = kin[...].astype(F32).T.astype(BF16)
 
-    last = jnp.minimum(N_DC - 1 - me, REACH)
-
-    def spread(r):
+    chip, core = me // 2, lax.rem(me, 2)
+    row, col = chip // COLS, lax.rem(chip, COLS)
+
+    def send(r, target, r_there, sem):
         return pltpu.make_async_remote_copy(
-            src_ref=slots.at[0, pl.ds(0, Z0), :], dst_ref=slots.at[r, pl.ds(0, Z0), :],
-            send_sem=spread_send.at[r], recv_sem=spread_recv.at[r],
-            device_id=(me + r, tp), device_id_type=MESH,
+            src_ref=slots.at[r, pl.ds(0, Z0), :], dst_ref=slots.at[r_there, pl.ds(0, Z0), :],
+            send_sem=sem, recv_sem=spread_recv.at[r_there], device_id=(target, tp), device_id_type=MESH,
         )
 
-    @pl.loop(1, last + 1)
-    def _(r):
-        spread(r).start()
+    def arrived(r):
+        here = slots.at[r, pl.ds(0, Z0), :]
+        pltpu.make_async_copy(here, here, spread_recv.at[r]).wait()
+
+    def down(j):
+        return (row >= j) & (row < ROWS_OF_CHIPS - 1), send(2 * COLS * j, me + 2 * COLS, 2 * COLS * (j + 1), down_send.at[j])
+
+    def along(j, step):
+        k = COLS * j + step
+        return (row >= j) & (col + step >= 0) & (col + step < COLS), send(
+            2 * COLS * j, me + 2 * step, 2 * k, along_send.at[j, step + COLS - 1]
+        )
+
+    def steps(j):
+        return [s for s in range(1 - COLS, COLS) if s and 0 < COLS * j + s <= REACH // 2]
+
+    def across(k):
+        found = []
+        if k < REACH // 2:
+            found.append((core == 0, send(2 * k, me + 1, 2 * k + 1, across_send.at[k])))
+        if k > 0:
+            found.append((core == 1, send(2 * k, me - 1, 2 * k - 1, across_send.at[k])))
+        return found
+
+    def start(copies):
+        for needed, copy in copies:
+            pl.when(needed)(copy.start)
+
+    def from_column(j):
+        if j:
+            pl.when(row >= j)(lambda: arrived(2 * COLS * j))
+        if j < REACH // 2 // COLS:
+            start([down(j)])
+        start([along(j, s) for s in steps(j)])
+        start([((row >= j) & core_ok, copy) for core_ok, copy in across(COLS * j)])
+
+    def from_row(j):
+        for s in steps(j):
+            k = COLS * j + s
+
+            @pl.when((row >= j) & (col - s >= 0) & (col - s < COLS))
+            def _():
+                arrived(2 * k)
+                start(across(k))
+
+    from_column(0)
 
     pltpu.make_async_copy(owners, owners, own_recv).wait()
     hits = jnp.where(owners[...].reshape(N_DC, ROWS) == me, 1.0, 0.0).astype(BF16)
@@ -155,11 +204,13 @@
 
     pltpu.make_async_copy(qin, qin, q_recv).wait()
 
+    for j in range(1, REACH // 2 // COLS + 1):
+        from_column(j)
+        from_row(j - 1)
+    from_row(REACH // 2 // COLS)
+
     def arrive(r):
-        @pl.when((r >= 1) & (r <= reach))
-        def _():
-            here = slots.at[r, pl.ds(0, Z0), :]
-            pltpu.make_async_copy(here, here, spread_recv.at[r]).wait()
+        pl.when((lax.rem(r, 2) == 1) & (r <= reach))(lambda: arrived(r))
 
     def key_pair(c):
         return jnp.concatenate([slots[2 * c, K0:END, :], slots[2 * c + 1, K0:END, :]], axis=1)
@@ -168,7 +219,7 @@
         queries = jnp.concatenate([qin[:, h * HEAD_DIM : (h + 1) * HEAD_DIM], neg[...]], axis=1)
         return jnp.dot(queries, keys, preferred_element_type=F32)
 
-    arrive(1)
+    arrive(jnp.int32(1))
     keys = key_pair(0)
     live = iota((ROWS, PAIR), 1) <= jnp.where(iota((ROWS, PAIR), 1) < ROWS, iota((ROWS, PAIR), 0), PAIR)
     for h in range(PER):
@@ -232,9 +283,20 @@
     sent = owners.at[pl.ds(0, N_DC - 1)]
     pltpu.make_async_copy(sent, sent, own_send).wait()
 
-    @pl.loop(1, last + 1)
-    def _(r):
-        spread(r).wait_send()
+    def left(copies):
+        for needed, copy in copies:
+            pl.when(needed)(copy.wait_send)
+
+    for j in range(REACH // 2 // COLS + 1):
+        if j < REACH // 2 // COLS:
+            left([down(j)])
+        left([along(j, s) for s in steps(j)])
+
+    @pl.loop(0, REACH // 2 + 1)
+    def _(k):
+        gone = slots.at[2 * k, pl.ds(0, Z0), :]
+        passed = (k <= chip) & jnp.where(core == 0, k < REACH // 2, k > 0)
+        pl.when(passed)(lambda: pltpu.make_async_copy(gone, gone, across_send.at[k]).wait())
 
     for g in range(PER // GROUP):
         sent = packed.at[g, pl.ds(0, (N_DC - 1) * TILE), :]
@@ -242,14 +304,14 @@
 
 
 def per_device(queries, keys, values, document_index, owner):
-    hbm = pl.BlockSpec(memory_space=pl.ANY)
+    hbm = pl.BlockSpec(memory_space=pltpu.HBM)
     vmem = pl.BlockSpec(memory_space=pltpu.VMEM)
     dma = pltpu.SemaphoreType.DMA
     groups = PER // GROUP
     return pl.pallas_call(
         kernel,
         out_shape=jax.ShapeDtypeStruct((ROWS, PER * HEAD_DIM), BF16),
-        in_specs=[hbm, hbm, hbm, vmem, vmem],
+        in_specs=[hbm] * 5,
         out_specs=vmem,
         scratch_shapes=[
             pltpu.VMEM((ROWS, HEAD_DIM), BF16),
@@ -264,7 +326,10 @@
             pltpu.VMEM((groups, N_DC * TILE, HEAD_DIM), BF16),
             pltpu.VMEM((groups, N_DC * TILE, HEAD_DIM), BF16),
             pltpu.VMEM((N_DC, 1, ROWS), I32),
-            dma((2,)), dma((2,)), dma, dma, dma, dma, dma((SLOTS,)), dma((SLOTS,)), dma((groups,)), dma((groups,)),
+            pltpu.VMEM((1, ROWS), I32),
+            pltpu.VMEM((1, ROWS), I32),
+            dma((2,)), dma((2,)), dma, dma, dma, dma, dma((2,)),
+            dma((4,)), dma((5, 7)), dma((REACH // 2 + 1,)), dma((SLOTS,)), dma((groups,)), dma((groups,)),
         ],
         compiler_params=pltpu.CompilerParams(
             collective_id=0, has_side_effects=True, vmem_limit_bytes=48 * 1024 * 1024

time: 146 us -> 70.1 us (0.48)
  Pallas kernels: 141 us -> 65.9 us
    pallas_call x1, Pallas kernels: 141 us -> 65.9 us  [per_device(): pl.pallas_call(kernel, out_shape=jax.ShapeDtypeStruct((ROWS, PER * HEAD_D...]
where the time goes in v2:
time: 70.1 us; the launch traced here: 69.8 us
  Pallas kernels  65.9 us (94%)
  local copies, waits for them, and re-layouts  3.84 us (5%)
    pallas_call x1, Pallas kernels, per_device(): pl.pallas_call(kernel, out_shape=jax.ShapeDtypeStruct((ROWS, PER * HEAD_D...  65.9 us
    unnamed x11, local copies, waits for them, and re-layouts  3.84 us

profile of v2, /device:TPU:1, one launch (start us, length us, event | category | flops | bytes accessed | tf_op | source)
XLA Modules:
  0.0 69.8 jit_solution(9896181527172491343)
XLA Ops:
  0.0 0.0 copy-start.3
  0.0 0.0 copy-start.4
  0.0 0.7 copy-done.3
  0.7 0.0 copy-done.4
  0.7 0.0 copy-start
  0.7 0.9 %copy-done = bf16[16,8192]{1,0:T(8,128)(2,1)S(1)} copy-done((bf16[16,8192]{1,0:T(8,128)(2,1)S(1)}, bf16[16,8192]{1,0:T(8,128)(2,1)}, u32[]{:S(2)}) %copy-start) | copy-done | bytes 262168
  1.6 0.0 copy-start.1
  1.6 0.8 %copy-done.1 = bf16[16,1024]{1,0:T(8,128)(2,1)S(1)} copy-done((bf16[16,1024]{1,0:T(8,128)(2,1)S(1)}, bf16[16,1024]{1,0:T(8,128)(2,1)}, u32[]{:S(2)}) %copy-start.1) | copy-done | bytes 32792
  2.4 0.0 copy-start.2
  2.4 0.8 %copy-done.2 = bf16[16,1024]{1,0:T(8,128)(2,1)S(1)} copy-done((bf16[16,1024]{1,0:T(8,128)(2,1)S(1)}, bf16[16,1024]{1,0:T(8,128)(2,1)}, u32[]{:S(2)}) %copy-start.2) | copy-done | bytes 32792
  3.1 65.9 %shard_map.55 = bf16[128,1024]{1,0:T(8,128)(2,1)S(1)} custom-call(bf16[16,8192]{1,0:T(8,128)(2,1)S(1)} %copy-done, bf16[16,1024]{1,0:T(8,128)(2,1)S(1)} %copy-done.1, bf16[16,1024]{1,0:T(8,128)(2,1)S(1)} %copy-done.2, s32[1,128]{1,0:T(1,128)S(1)} %bitcast.2, s32[1,128]{1,0:T(1,128)S(1)} %bitcast.3), custom_call_target="tpu_custom_call" | custom-call | flops 2300000000 | bytes 4000000 | tf_op jit(solution)/shard_map/pallas_call | solution.py:311
  69.1 0.7 %copy.7 = bf16[128,1024]{1,0:T(8,128)(2,1)} copy(bf16[128,1024]{1,0:T(8,128)(2,1)S(1)} %shard_map.55) | data formatting | bytes 524288
Async XLA Ops:
  0.0 0.7 copy-start.3
  0.0 0.7 copy-start.4
  0.7 0.9 %copy-start = (bf16[16,8192]{1,0:T(8,128)(2,1)S(1)}, bf16[16,8192]{1,0:T(8,128)(2,1)}, u32[]{:S(2)}) copy-start(bf16[16,8192]{1,0:T(8,128)(2,1)} %q_hbm.1) | copy-start | bytes 786436
  1.6 0.8 %copy-start.1 = (bf16[16,1024]{1,0:T(8,128)(2,1)S(1)}, bf16[16,1024]{1,0:T(8,128)(2,1)}, u32[]{:S(2)}) copy-start(bf16[16,1024]{1,0:T(8,128)(2,1)} %k_hbm.1) | copy-start | bytes 98308
  2.4 0.8 %copy-start.2 = (bf16[16,1024]{1,0:T(8,128)(2,1)S(1)}, bf16[16,1024]{1,0:T(8,128)(2,1)}, u32[]{:S(2)}) copy-start(bf16[16,1024]{1,0:T(8,128)(2,1)} %v_hbm.1) | copy-start | bytes 98308

commit v3 on v2

v3 whole, which is shorter than its diff:
```python
import functools
import math

import jax
import jax.numpy as jnp
from jax import lax
from jax.experimental import pallas as pl
from jax.experimental.pallas import tpu as pltpu
from jax.sharding import PartitionSpec as P

MESH = pl.DeviceIdType.MESH
HEADS = 64
KVH = 8
HEAD_DIM = 128
ROWS = 128
N_DC = 64
N_TP = 8
ROWS_OF_CHIPS, COLS = 8, 4
PER = HEADS // KVH
REACH = 32
SLOTS = 34
STEP = 8
CAP = 4
GROUP = 4
TILE = CAP * GROUP
DEAD = -1e30
V0, K0, D0, Z0, END = 0, 128, 256, 272, 384
PARTS = ((K0, Z0), (V0, K0))
VALUES = 1
SCALE = math.log2(math.e) / math.sqrt(HEAD_DIM)
F32, BF16, I32 = jnp.float32, jnp.bfloat16, jnp.int32


def iota(shape, dim):
    return lax.broadcasted_iota(I32, shape, dim)


def kernel(
    q_hbm, k_hbm, v_hbm, doc_hbm, own_hbm, out_ref,
    kin, qin, slots, neg, queries, peak, totals, weighted, pack, unpack, packed, got, owners, doc_ref, own_ref,
    kv_send, kv_recv, q_send, q_recv, own_send, own_recv, doc_sem, down_send, along_send, across_send, spread_recv, out_send, out_recv, heard,
):
    me = lax.axis_index("dc")
    tp = lax.axis_index("tp")

    pltpu.make_async_copy(doc_hbm, doc_ref, doc_sem.at[0]).start()
    pltpu.make_async_copy(own_hbm, own_ref, doc_sem.at[1]).start()
    chip, core = me // 2, lax.rem(me, 2)
    row, col = chip // COLS, lax.rem(chip, COLS)
    sibling = me + 1 - 2 * core

    def rows_on(n):
        return lax.rem(row + n + ROWS_OF_CHIPS, ROWS_OF_CHIPS) * 2 * COLS + 2 * col + core

    def greet(semaphore, device):
        pl.semaphore_signal(semaphore, inc=1, device_id=device, device_id_type=MESH)

    barrier = pltpu.get_barrier_semaphore()

    @pl.loop(1, N_TP)
    def _(j):
        greet(barrier, (me, lax.rem(tp + j, N_TP)))

    greet(barrier, (sibling, tp))
    for n in range(1, COLS):
        greet(barrier, (row * 2 * COLS + 2 * lax.rem(col + n, COLS) + core, tp))
    for n in (-1, 1):
        greet(barrier, (rows_on(n), tp))
    pl.semaphore_wait(barrier, N_TP - 1 + 1 + COLS - 1 + 2)

    def tell(stage):
        if stage == 0:
            greet(heard.at[0], (sibling, tp))
        elif stage == 3:
            greet(heard.at[3], (rows_on(4), tp))
        else:
            greet(heard.at[stage], (rows_on(stage), tp))
            greet(heard.at[stage], (rows_on(-stage), tp))

    def hear(stage):
        pl.semaphore_wait(heard.at[stage], 2 if stage in (1, 2) else 1)

    tell(0)

    mine = pl.ds(pl.multiple_of(tp * 16, 16), 16)

    def columns(t, width):
        return pl.ds(pl.multiple_of(t * width, width), width)

    def part(source, t, width, target, send, recv):
        return pltpu.make_async_remote_copy(
            src_ref=source.at[:, columns(t, width)], dst_ref=target, send_sem=send, recv_sem=recv,
            device_id=(me, t), device_id_type=MESH,
        )

    value_target = slots.at[0, pl.ds(pl.multiple_of(V0 + tp * 16, 16), 16), :]

    @pl.loop(1, N_TP)
    def _(j):
        t = lax.rem(tp + j, N_TP)
        part(k_hbm, t, HEAD_DIM, kin.at[mine, :], kv_send.at[0], kv_recv.at[0]).start()
        part(v_hbm, t, HEAD_DIM, value_target, kv_send.at[1], kv_recv.at[1]).start()

    pltpu.make_async_copy(k_hbm.at[:, columns(tp, HEAD_DIM)], kin.at[mine, :], kv_recv.at[0]).start()
    pltpu.make_async_copy(v_hbm.at[:, columns(tp, HEAD_DIM)], value_target, kv_recv.at[1]).start()

    @pl.loop(1, N_TP)
    def _(j):
        t = lax.rem(tp + j, N_TP)
        part(q_hbm, t, PER * HEAD_DIM, qin.at[mine, :], q_send, q_recv).start()

    pltpu.make_async_copy(q_hbm.at[:, columns(tp, PER * HEAD_DIM)], qin.at[mine, :], q_recv).start()

    slots[:, Z0:END, :] = jnp.zeros((SLOTS, END - Z0, ROWS), BF16)
    reach = jnp.minimum(me, REACH)

    @pl.loop(reach + 1, jnp.minimum((reach // STEP + 1) * STEP, SLOTS))
    def _(r):
        slots[r, V0:D0, :] = jnp.zeros((D0 - V0, ROWS), BF16)
        slots[r, D0:Z0, :] = jnp.ones((Z0 - D0, ROWS), BF16)

    pltpu.make_async_copy(doc_hbm, doc_ref, doc_sem.at[0]).wait()
    doc = doc_ref[...]
    slots[0, D0:Z0, :] = jnp.where(iota((Z0 - D0, ROWS), 0) == doc, 1.0, 0.0).astype(BF16)
    other = jnp.where((iota((ROWS, ROWS), 0) != doc) & (iota((ROWS, ROWS), 0) < Z0 - D0), DEAD, 0.0)
    neg[...] = other.T.astype(BF16)

    pltpu.make_async_copy(own_hbm, own_ref, doc_sem.at[1]).wait()
    owner = own_ref[...]
    owner_col = jnp.broadcast_to(owner, (ROWS, ROWS)).astype(F32).T
    same = (owner_col == owner.astype(F32)) & (iota((ROWS, ROWS), 0) < iota((ROWS, ROWS), 1))
    rank = jnp.sum(jnp.where(same, 1.0, 0.0), axis=0, keepdims=True).astype(I32)
    place = owner * TILE + rank
    target = jnp.concatenate([place + h * CAP for h in range(GROUP)], axis=1)

    @pl.loop(0, N_DC * TILE, step=128)
    def _(base):
        base = pl.multiple_of(base, 128)
        rows = iota((128, GROUP * ROWS), 0) + base
        pack[pl.ds(base, 128), :] = jnp.where(rows == target, 1.0, 0.0).astype(BF16)

    hear(0)
    tell(1)

    pltpu.make_async_copy(kin, kin, kv_recv.at[0]).wait()
    slots[0, K0:D0, :] = kin[...].astype(F32).T.astype(BF16)

    def rows_of(r, p):
        return slots.at[r, pl.ds(PARTS[p][0], PARTS[p][1] - PARTS[p][0]), :]

    def send(r, target, r_there, sem, p):
        return pltpu.make_async_remote_copy(
            src_ref=rows_of(r, p), dst_ref=rows_of(r_there, p), send_sem=sem.at[p],
            recv_sem=spread_recv.at[r_there, p], device_id=(target, tp), device_id_type=MESH,
        )

    def arrived(r, p):
        pltpu.make_async_copy(rows_of(r, p), rows_of(r, p), spread_recv.at[r, p]).wait()

    def down(j, p):
        there = 2 * COLS * (j + 1)
        return (row >= j) & (row < ROWS_OF_CHIPS - 1), send(2 * COLS * j, me + 2 * COLS, there, down_send.at[j], p)

    def along(j, step, p):
        k = COLS * j + step
        return (row >= j) & (col + step >= 0) & (col + step < COLS), send(
            2 * COLS * j, me + 2 * step, 2 * k, along_send.at[j, step + COLS - 1], p
        )

    def steps(j):
        return [s for s in range(1 - COLS, COLS) if s and 0 < COLS * j + s <= REACH // 2]

    def across(k, p):
        found = []
        if k < REACH // 2:
            found.append((core == 0, send(2 * k, me + 1, 2 * k + 1, across_send.at[k], p)))
        if k > 0:
            found.append((core == 1, send(2 * k, me - 1, 2 * k - 1, across_send.at[k], p)))
        return found

    def start(copies):
        for needed, copy in copies:
            pl.when(needed)(copy.start)

    def from_column(j):
        for p in range(len(PARTS)):
            if j:
                pl.when(row >= j)(functools.partial(arrived, 2 * COLS * j, p))
            elif p == VALUES:
                pltpu.make_async_copy(kin, kin, kv_recv.at[1]).wait()
            if j < REACH // 2 // COLS:
                start([down(j, p)])
            start([along(j, s, p) for s in steps(j)])
            start([((row >= j) & its_core, copy) for its_core, copy in across(COLS * j, p)])

    def from_row(j):
        for p in range(len(PARTS)):
            for s in steps(j):
                k = COLS * j + s

                @pl.when((row >= j) & (col - s >= 0) & (col - s < COLS))
                def _():
                    arrived(2 * k, p)
                    start(across(k, p))

    from_column(0)

    def arrive(r):
        @pl.when((lax.rem(r, 2) == 1) & (r <= reach))
        def _():
            for p in range(len(PARTS)):
                arrived(r, p)

    def attend(step, group):
        base = step * STEP
        count = min(STEP, SLOTS - base)
        at = pl.ds(group * GROUP * ROWS, GROUP * ROWS)
        keys = jnp.concatenate([slots[base + i, K0:END, :] for i in range(count)], axis=1)
        values = jnp.concatenate([slots[base + i, V0:K0, :] for i in range(count)], axis=0)
        s = jnp.dot(queries[at, :], keys, preferred_element_type=F32)
        s = [s[:, i * ROWS : (i + 1) * ROWS] for i in range(count)]
        if step == 0:
            row_of = lax.rem(iota((GROUP * ROWS, ROWS), 0), ROWS)
            s[0] = jnp.where(iota((GROUP * ROWS, ROWS), 1) <= row_of, s[0], DEAD)
        top = jnp.max(functools.reduce(jnp.maximum, s), axis=1, keepdims=True)
        if step == 0:
            top = jnp.broadcast_to(top, (GROUP * ROWS, ROWS))
        else:
            old = peak[at, :]
            top = jnp.maximum(old, top)
            shrink = jnp.exp2((old - top) * SCALE)
        weights = [jnp.exp2((x - top) * SCALE) for x in s]
        total = functools.reduce(jnp.add, weights)
        rounded = jnp.concatenate([w.astype(BF16) for w in weights], axis=1)
        summed = jnp.dot(rounded, values, preferred_element_type=F32)
        if step > 0:
            total = totals[at, :] * shrink + total
            summed = weighted[at, :] * shrink + summed
        peak[at, :] = top
        totals[at, :] = total
        weighted[at, :] = summed

    def step_of(step, groups):
        def run():
            for i in range(1, min(STEP, SLOTS - step * STEP), 2):
                if groups[0] == 0:
                    arrive(jnp.int32(step * STEP + i))
            for g in groups:
                attend(step, g)

        if step:
            pl.when(reach >= step * STEP)(run)
        else:
            run()

    every = tuple(range(PER // GROUP))
    from_column(1)
    hear(1)
    tell(2)
    from_row(0)
    from_column(2)
    hear(2)
    tell(3)
    from_row(1)
    from_column(3)
    from_row(2)
    hear(3)

    @pl.loop(1, N_DC)
    def _(j):
        pltpu.make_async_remote_copy(
            src_ref=own_ref, dst_ref=owners.at[me], send_sem=own_send, recv_sem=own_recv,
            device_id=(lax.rem(me + j, N_DC), tp), device_id_type=MESH,
        ).start()

    pltpu.make_async_copy(own_ref, owners.at[me], own_recv).start()

    pltpu.make_async_copy(qin, qin, q_recv).wait()
    for h in range(PER):
        queries[h * ROWS : (h + 1) * ROWS, :HEAD_DIM] = qin[:, h * HEAD_DIM : (h + 1) * HEAD_DIM]
        queries[h * ROWS : (h + 1) * ROWS, HEAD_DIM:] = neg[...]
    step_of(0, every)
    from_column(4)
    from_row(3)
    step_of(1, every)
    from_row(4)
    step_of(2, every)

    for g in every:
        step_of(3, (g,))
        step_of(4, (g,))
        at = pl.ds(g * GROUP * ROWS, GROUP * ROWS)
        context = (weighted[at, :] / jnp.sum(totals[at, :], axis=1, keepdims=True)).astype(BF16)
        packed[g] = jnp.dot(pack[...], context, preferred_element_type=F32).astype(BF16)

        def tile(r):
            return pl.ds(pl.multiple_of(r * TILE, TILE), TILE)

        @pl.loop(1, N_DC)
        def _(j):
            to = lax.rem(me + j, N_DC)
            pltpu.make_async_remote_copy(
                src_ref=packed.at[g, tile(to), :], dst_ref=got.at[g, tile(me), :],
                send_sem=out_send.at[g], recv_sem=out_recv.at[g], device_id=(to, tp), device_id_type=MESH,
            ).start()

        pltpu.make_async_copy(packed.at[g, tile(me), :], got.at[g, tile(me), :], out_recv.at[g]).start()

    pltpu.make_async_copy(owners, owners, own_recv).wait()
    hits = jnp.where(owners[...].reshape(N_DC, ROWS) == me, 1.0, 0.0).astype(BF16)
    counts = lax.dot_general(
        jnp.ones((8, ROWS), BF16), hits, (((1,), (1,)), ((), ())), preferred_element_type=F32
    ).astype(BF16)
    lane_source = iota((N_DC, N_DC * TILE), 1) // TILE
    row_source = iota((N_DC, N_DC * TILE), 0)
    count = jnp.dot(counts, jnp.where(lane_source == row_source, 1.0, 0.0).astype(BF16), preferred_element_type=F32)
    before = jnp.dot(counts, jnp.where(row_source < lane_source, 1.0, 0.0).astype(BF16), preferred_element_type=F32)
    lane = iota((1, N_DC * TILE), 1)
    turn = lane % CAP
    goal = jnp.where(
        turn < count[0:1].astype(I32), before[0:1].astype(I32) + turn + (lane // CAP % GROUP) * ROWS, -1
    )

    @pl.loop(0, GROUP * ROWS, step=64)
    def _(base):
        base = pl.multiple_of(base, 64)
        rows = iota((64, N_DC * TILE), 0) + base
        unpack[pl.ds(base, 64), :] = jnp.where(rows == goal, 1.0, 0.0).astype(BF16)

    for g in range(PER // GROUP):
        pltpu.make_async_copy(got.at[g], got.at[g], out_recv.at[g]).wait()
        rows = jnp.dot(unpack[...], got[g], preferred_element_type=F32).astype(BF16)
        for i in range(GROUP):
            h = g * GROUP + i
            out_ref[:, h * HEAD_DIM : (h + 1) * HEAD_DIM] = rows[i * ROWS : (i + 1) * ROWS]

    seven = kin.at[pl.ds(0, ROWS - 16), :]
    pltpu.make_async_copy(seven, seven, kv_send.at[0]).wait()
    pltpu.make_async_copy(seven, seven, kv_send.at[1]).wait()
    sent = qin.at[pl.ds(0, ROWS - 16), :]
    pltpu.make_async_copy(sent, sent, q_send).wait()
    sent = owners.at[pl.ds(0, N_DC - 1)]
    pltpu.make_async_copy(sent, sent, own_send).wait()

    def left(copies):
        for needed, copy in copies:
            pl.when(needed)(copy.wait_send)

    for p in range(len(PARTS)):
        for j in range(REACH // 2 // COLS + 1):
            if j < REACH // 2 // COLS:
                left([down(j, p)])
            left([along(j, s, p) for s in steps(j)])

        @pl.loop(0, REACH // 2 + 1)
        def _(k):
            gone = rows_of(2 * k, p)
            passed = (k <= chip) & jnp.where(core == 0, k < REACH // 2, k > 0)
            pl.when(passed)(lambda: pltpu.make_async_copy(gone, gone, across_send.at[k, p]).wait())

    for g in range(PER // GROUP):
        sent = packed.at[g, pl.ds(0, (N_DC - 1) * TILE), :]
        pltpu.make_async_copy(sent, sent, out_send.at[g]).wait()


def per_device(queries, keys, values, document_index, owner):
    hbm = pl.BlockSpec(memory_space=pltpu.HBM)
    vmem = pl.BlockSpec(memory_space=pltpu.VMEM)
    dma = pltpu.SemaphoreType.DMA
    groups, parts = PER // GROUP, len(PARTS)
    return pl.pallas_call(
        kernel,
        out_shape=jax.ShapeDtypeStruct((ROWS, PER * HEAD_DIM), BF16),
        in_specs=[hbm] * 5,
        out_specs=vmem,
        scratch_shapes=[
            pltpu.VMEM((ROWS, HEAD_DIM), BF16),
            pltpu.VMEM((ROWS, PER * HEAD_DIM), BF16),
            pltpu.VMEM((SLOTS, END, ROWS), BF16),
            pltpu.VMEM((ROWS, ROWS), BF16),
            pltpu.VMEM((PER * ROWS, 2 * HEAD_DIM), BF16),
            pltpu.VMEM((PER * ROWS, ROWS), F32),
            pltpu.VMEM((PER * ROWS, ROWS), F32),
            pltpu.VMEM((PER * ROWS, HEAD_DIM), F32),
            pltpu.VMEM((N_DC * TILE, GROUP * ROWS), BF16),
            pltpu.VMEM((GROUP * ROWS, N_DC * TILE), BF16),
            pltpu.VMEM((groups, N_DC * TILE, HEAD_DIM), BF16),
            pltpu.VMEM((groups, N_DC * TILE, HEAD_DIM), BF16),
            pltpu.VMEM((N_DC, 1, ROWS), I32),
            pltpu.VMEM((1, ROWS), I32),
            pltpu.VMEM((1, ROWS), I32),
            dma((2,)), dma((2,)), dma, dma, dma, dma, dma((2,)),
            dma((4, parts)), dma((5, 7, parts)), dma((REACH // 2 + 1, parts)), dma((SLOTS, parts)), dma((groups,)), dma((groups,)),
            pltpu.SemaphoreType.REGULAR((4,)),
        ],
        compiler_params=pltpu.CompilerParams(
            collective_id=0, has_side_effects=True, vmem_limit_bytes=63 * 1024 * 1024
        ),
        cost_estimate=pl.CostEstimate(flops=2_300_000_000, bytes_accessed=4_000_000, transcendentals=4_500_000),
    )(queries, keys, values, document_index.reshape(1, ROWS), owner.reshape(1, ROWS))


def solution(mesh):
    return jax.shard_map(
        per_device,
        mesh=mesh,
        in_specs=(
            P(("dc", "tp"), None),
            P(("dc", "tp"), None),
            P(("dc", "tp"), None),
            P("dc"),
            P("dc"),
        ),
        out_specs=P("dc", "tp"),
        check_vma=False,
    )
```

time: 70.1 us -> 63.8 us (0.910)
  Pallas kernels: 65.9 us -> 62 us
  local copies, waits for them, and re-layouts: 3.84 us -> 1.67 us
    pallas_call x1, Pallas kernels: 65.9 us -> 62 us  [per_device(): pl.pallas_call(kernel, out_shape=jax.ShapeDtypeStruct((ROWS, PER * HEAD_D...]
    unnamed x11 -> x1, local copies, waits for them, and re-layouts: 3.84 us -> 1.67 us
where the time goes in v3:
time: 63.8 us; the launch traced here: 63.7 us
  Pallas kernels  62 us (97%)
  local copies, waits for them, and re-layouts  1.67 us (3%)
    pallas_call x1, Pallas kernels, per_device(): pl.pallas_call(kernel, out_shape=jax.ShapeDtypeStruct((ROWS, PER * HEAD_D...  62 us
    unnamed x1, local copies, waits for them, and re-layouts  1.67 us

profile of v3, /device:TPU:1, one launch (start us, length us, event | category | flops | bytes accessed | tf_op | source)
XLA Modules:
  0.0 63.7 jit_solution(10208724505634014699)
XLA Ops:
  0.0 62.0 %shard_map.55 = bf16[128,1024]{1,0:T(8,128)(2,1)} custom-call(bf16[16,8192]{1,0:T(8,128)(2,1)} %q_hbm.1, bf16[16,1024]{1,0:T(8,128)(2,1)} %k_hbm.1, bf16[16,1024]{1,0:T(8,128)(2,1)} %v_hbm.1, s32[1,128]{1,0:T(1,128)} %bitcast.2, s32[1,128]{1,0:T(1,128)} %bitcast.3), custom_call_target="tpu_custom_call" | custom-call | flops 2300000000 | bytes 4000000 | tf_op jit(solution)/shard_map/pallas_call | solution.py:371
  62.0 1.7 %copy.7 = bf16[128,1024]{1,0:T(8,128)(2,1)} copy(bf16[128,1024]{1,0:T(8,128)(2,1)} %shard_map.55) | data formatting | bytes 524288

commit v4 on v3

--- a/solution.py
+++ b/solution.py
@@ -16,6 +16,7 @@
 N_DC = 64
 N_TP = 8
 ROWS_OF_CHIPS, COLS = 8, 4
+CHIPS = ROWS_OF_CHIPS * COLS
 PER = HEADS // KVH
 REACH = 32
 SLOTS = 34
@@ -26,6 +27,7 @@
 DEAD = -1e30
 V0, K0, D0, Z0, END = 0, 128, 256, 272, 384
 PARTS = ((K0, Z0), (V0, K0))
+DOWN = {0: (1,), 1: (1,), 2: (1,), 3: (1,)}
 VALUES = 1
 SCALE = math.log2(math.e) / math.sqrt(HEAD_DIM)
 F32, BF16, I32 = jnp.float32, jnp.bfloat16, jnp.int32
@@ -37,8 +39,8 @@
 
 def kernel(
     q_hbm, k_hbm, v_hbm, doc_hbm, own_hbm, out_ref,
-    kin, qin, slots, neg, queries, peak, totals, weighted, pack, unpack, packed, got, owners, doc_ref, own_ref,
-    kv_send, kv_recv, q_send, q_recv, own_send, own_recv, doc_sem, down_send, along_send, across_send, spread_recv, out_send, out_recv, heard,
+    kin, qin, slots, neg, queries, peak, totals, weighted, pack, unpack, packed, landed, handed, attended, owners, places, doc_ref, own_ref,
+    kv_send, kv_recv, q_send, q_recv, own_send, own_recv, place_send, place_recv, doc_sem, down_send, below_send, along_send, across_send, spread_recv, out_send, out_recv, hand_send, hand_recv, out_sem, heard,
 ):
     me = lax.axis_index("dc")
     tp = lax.axis_index("tp")
@@ -69,16 +71,14 @@
     pl.semaphore_wait(barrier, N_TP - 1 + 1 + COLS - 1 + 2)
 
     def tell(stage):
-        if stage == 0:
-            greet(heard.at[0], (sibling, tp))
-        elif stage == 3:
-            greet(heard.at[3], (rows_on(4), tp))
+        if stage == 2:
+            greet(heard.at[2], (rows_on(4), tp))
         else:
-            greet(heard.at[stage], (rows_on(stage), tp))
-            greet(heard.at[stage], (rows_on(-stage), tp))
+            greet(heard.at[stage], (rows_on(stage + 1), tp))
+            greet(heard.at[stage], (rows_on(-stage - 1), tp))
 
     def hear(stage):
-        pl.semaphore_wait(heard.at[stage], 2 if stage in (1, 2) else 1)
+        pl.semaphore_wait(heard.at[stage], 1 if stage == 2 else 2)
 
     tell(0)
 
@@ -158,8 +158,12 @@
         pltpu.make_async_copy(rows_of(r, p), rows_of(r, p), spread_recv.at[r, p]).wait()
 
     def down(j, p):
-        there = 2 * COLS * (j + 1)
-        return (row >= j) & (row < ROWS_OF_CHIPS - 1), send(2 * COLS * j, me + 2 * COLS, there, down_send.at[j], p)
+        found = []
+        for n in DOWN.get(j, ()):
+            there = 2 * COLS * (j + n)
+            copy = send(2 * COLS * j, me + 2 * COLS * n, there, down_send.at[j + n - 1], p)
+            found.append(((row >= j) & (row + n < ROWS_OF_CHIPS), copy))
+        return found
 
     def along(j, step, p):
         k = COLS * j + step
@@ -169,6 +173,19 @@
 
     def steps(j):
         return [s for s in range(1 - COLS, COLS) if s and 0 < COLS * j + s <= REACH // 2]
+
+    def sideways(j):
+        return [s for s in steps(j) if abs(s) != 2 or j < 2]
+
+    def below(j, p):
+        found = []
+        for s in (2, -2):
+            k = COLS * j + s
+            if j and k + COLS <= REACH // 2:
+                copy = send(2 * k, me + 2 * COLS, 2 * (k + COLS), below_send.at[j], p)
+                there = (row >= j) & (row < ROWS_OF_CHIPS - 1) & (col - s >= 0) & (col - s < COLS)
+                found.append((there, copy))
+        return found
 
     def across(k, p):
         found = []
@@ -188,22 +205,66 @@
                 pl.when(row >= j)(functools.partial(arrived, 2 * COLS * j, p))
             elif p == VALUES:
                 pltpu.make_async_copy(kin, kin, kv_recv.at[1]).wait()
-            if j < REACH // 2 // COLS:
-                start([down(j, p)])
-            start([along(j, s, p) for s in steps(j)])
+            start(down(j, p))
+            start([along(j, s, p) for s in sideways(j)])
             start([((row >= j) & its_core, copy) for its_core, copy in across(COLS * j, p)])
 
     def from_row(j):
         for p in range(len(PARTS)):
-            for s in steps(j):
+            for s in sorted(steps(j), key=lambda s: abs(s) != 2):
                 k = COLS * j + s
 
                 @pl.when((row >= j) & (col - s >= 0) & (col - s < COLS))
                 def _():
                     arrived(2 * k, p)
+                    if abs(s) == 2:
+                        start(below(j, p))
                     start(across(k, p))
 
     from_column(0)
+
+    def send_owner():
+        for i in range(COLS):
+            there = tp * COLS + i
+            pl.when(there != chip)(pltpu.make_async_remote_copy(
+                src_ref=own_ref, dst_ref=owners.at[core, chip], send_sem=own_send.at[i], recv_sem=own_recv.at[0],
+                device_id=(2 * there + core, tp), device_id_type=MESH,
+            ).start)
+        pl.when(row == tp)(pltpu.make_async_copy(own_ref, owners.at[core, chip], own_recv.at[0]).start)
+
+    def swap_owners():
+        return pltpu.make_async_remote_copy(
+            src_ref=owners.at[core], dst_ref=owners.at[core], send_sem=own_send.at[COLS], recv_sem=own_recv.at[1],
+            device_id=(sibling, tp), device_id_type=MESH,
+        )
+
+    def gather_owners():
+        pltpu.make_async_copy(owners.at[core], owners.at[core], own_recv.at[0]).wait()
+        swap_owners().start()
+
+    def send_places():
+        swap_owners().wait()
+        hits = jnp.where(owners[...].reshape(N_DC, ROWS) == me, 1.0, 0.0).astype(BF16)
+        counts = lax.dot_general(
+            jnp.ones((8, ROWS), BF16), hits, (((1,), (1,)), ((), ())), preferred_element_type=F32
+        ).astype(BF16)
+        lane = iota((1, N_DC * TILE), 1)
+        turn = lax.rem(lane, CAP)
+        from_core = jnp.where(lane < N_DC * TILE // 2, core, 1 - core)
+        source = 2 * lax.rem(lane // TILE, CHIPS) + from_core
+        listed = iota((N_DC, N_DC * TILE), 0)
+        listed = 2 * lax.rem(listed, CHIPS) + listed // CHIPS
+        count = jnp.dot(counts, jnp.where(listed == source, 1.0, 0.0).astype(BF16), preferred_element_type=F32)
+        before = jnp.dot(counts, jnp.where(listed < source, 1.0, 0.0).astype(BF16), preferred_element_type=F32)
+        head = lax.rem(lane // CAP, GROUP)
+        places[...] = jnp.where(turn < count[0:1].astype(I32), before[0:1].astype(I32) + turn + head * ROWS, -1)
+
+        @pl.loop(1, N_TP)
+        def _(j):
+            pltpu.make_async_remote_copy(
+                src_ref=places, dst_ref=places, send_sem=place_send.at[j], recv_sem=place_recv,
+                device_id=(me, lax.rem(tp + j, N_TP)), device_id_type=MESH,
+            ).start()
 
     def arrive(r):
         @pl.when((lax.rem(r, 2) == 1) & (r <= reach))
@@ -259,32 +320,26 @@
     tell(2)
     from_row(0)
     from_column(2)
+    from_row(1)
     hear(2)
-    tell(3)
-    from_row(1)
+    send_owner()
     from_column(3)
-    from_row(2)
-    hear(3)
-
-    @pl.loop(1, N_DC)
-    def _(j):
-        pltpu.make_async_remote_copy(
-            src_ref=own_ref, dst_ref=owners.at[me], send_sem=own_send, recv_sem=own_recv,
-            device_id=(lax.rem(me + j, N_DC), tp), device_id_type=MESH,
-        ).start()
-
-    pltpu.make_async_copy(own_ref, owners.at[me], own_recv).start()
-
     pltpu.make_async_copy(qin, qin, q_recv).wait()
     for h in range(PER):
         queries[h * ROWS : (h + 1) * ROWS, :HEAD_DIM] = qin[:, h * HEAD_DIM : (h + 1) * HEAD_DIM]
         queries[h * ROWS : (h + 1) * ROWS, HEAD_DIM:] = neg[...]
-    step_of(0, every)
+    step_of(0, (0,))
+    from_row(2)
+    step_of(0, (1,))
     from_column(4)
+    step_of(1, (0,))
     from_row(3)
-    step_of(1, every)
+    pl.when(row == tp)(gather_owners)
+    step_of(1, (1,))
+    step_of(2, (0,))
+    step_of(2, (1,))
+    pl.when(row == tp)(send_places)
     from_row(4)
-    step_of(2, every)
 
     for g in every:
         step_of(3, (g,))
@@ -293,33 +348,24 @@
         context = (weighted[at, :] / jnp.sum(totals[at, :], axis=1, keepdims=True)).astype(BF16)
         packed[g] = jnp.dot(pack[...], context, preferred_element_type=F32).astype(BF16)
 
-        def tile(r):
-            return pl.ds(pl.multiple_of(r * TILE, TILE), TILE)
-
-        @pl.loop(1, N_DC)
+        def two(c):
+            return packed.at[g, pl.ds(pl.multiple_of(c * 2 * TILE, 2 * TILE), 2 * TILE), :]
+
+        @pl.loop(1, CHIPS)
         def _(j):
-            to = lax.rem(me + j, N_DC)
+            to = lax.rem(chip + j, CHIPS)
             pltpu.make_async_remote_copy(
-                src_ref=packed.at[g, tile(to), :], dst_ref=got.at[g, tile(me), :],
-                send_sem=out_send.at[g], recv_sem=out_recv.at[g], device_id=(to, tp), device_id_type=MESH,
+                src_ref=two(to), dst_ref=landed.at[g, chip], send_sem=out_send.at[g], recv_sem=out_recv.at[g],
+                device_id=(2 * to + core, tp), device_id_type=MESH,
             ).start()
 
-        pltpu.make_async_copy(packed.at[g, tile(me), :], got.at[g, tile(me), :], out_recv.at[g]).start()
-
-    pltpu.make_async_copy(owners, owners, own_recv).wait()
-    hits = jnp.where(owners[...].reshape(N_DC, ROWS) == me, 1.0, 0.0).astype(BF16)
-    counts = lax.dot_general(
-        jnp.ones((8, ROWS), BF16), hits, (((1,), (1,)), ((), ())), preferred_element_type=F32
-    ).astype(BF16)
-    lane_source = iota((N_DC, N_DC * TILE), 1) // TILE
-    row_source = iota((N_DC, N_DC * TILE), 0)
-    count = jnp.dot(counts, jnp.where(lane_source == row_source, 1.0, 0.0).astype(BF16), preferred_element_type=F32)
-    before = jnp.dot(counts, jnp.where(row_source < lane_source, 1.0, 0.0).astype(BF16), preferred_element_type=F32)
-    lane = iota((1, N_DC * TILE), 1)
-    turn = lane % CAP
-    goal = jnp.where(
-        turn < count[0:1].astype(I32), before[0:1].astype(I32) + turn + (lane // CAP % GROUP) * ROWS, -1
-    )
+        pltpu.make_async_copy(two(chip), landed.at[g, chip], out_recv.at[g]).start()
+
+    @pl.when(row != tp)
+    def _():
+        pltpu.make_async_copy(places, places, place_recv).wait()
+
+    goal = places[...]
 
     @pl.loop(0, GROUP * ROWS, step=64)
     def _(base):
@@ -327,20 +373,44 @@
         rows = iota((64, N_DC * TILE), 0) + base
         unpack[pl.ds(base, 64), :] = jnp.where(rows == goal, 1.0, 0.0).astype(BF16)
 
-    for g in range(PER // GROUP):
-        pltpu.make_async_copy(got.at[g], got.at[g], out_recv.at[g]).wait()
-        rows = jnp.dot(unpack[...], got[g], preferred_element_type=F32).astype(BF16)
+    def hand(g):
+        its = pl.ds(pl.multiple_of((1 - core) * TILE, TILE), TILE)
+        return pltpu.make_async_remote_copy(
+            src_ref=landed.at[g, :, its, :], dst_ref=handed.at[g], send_sem=hand_send.at[g], recv_sem=hand_recv.at[g],
+            device_id=(sibling, tp), device_id_type=MESH,
+        )
+
+    def written(g):
+        part_of = pl.ds(g * GROUP * HEAD_DIM, GROUP * HEAD_DIM)
+        return pltpu.make_async_copy(attended.at[:, part_of], out_ref.at[:, part_of], out_sem.at[g])
+
+    ours = pl.ds(pl.multiple_of(core * TILE, TILE), TILE)
+    for g in every:
+        pltpu.make_async_copy(landed.at[g], landed.at[g], out_recv.at[g]).wait()
+        hand(g).start()
+        half = N_DC * TILE // 2
+        rows = jnp.dot(unpack[:, :half], landed[g, :, ours, :].reshape(half, HEAD_DIM), preferred_element_type=F32)
+        hand(g).wait_recv()
+        rows = rows + jnp.dot(unpack[:, half:], handed[g].reshape(half, HEAD_DIM), preferred_element_type=F32)
+        rows = rows.astype(BF16)
         for i in range(GROUP):
             h = g * GROUP + i
-            out_ref[:, h * HEAD_DIM : (h + 1) * HEAD_DIM] = rows[i * ROWS : (i + 1) * ROWS]
+            attended[:, h * HEAD_DIM : (h + 1) * HEAD_DIM] = rows[i * ROWS : (i + 1) * ROWS]
+        written(g).start()
 
     seven = kin.at[pl.ds(0, ROWS - 16), :]
     pltpu.make_async_copy(seven, seven, kv_send.at[0]).wait()
     pltpu.make_async_copy(seven, seven, kv_send.at[1]).wait()
     sent = qin.at[pl.ds(0, ROWS - 16), :]
     pltpu.make_async_copy(sent, sent, q_send).wait()
-    sent = owners.at[pl.ds(0, N_DC - 1)]
-    pltpu.make_async_copy(sent, sent, own_send).wait()
+    for i in range(COLS):
+        pl.when(tp * COLS + i != chip)(pltpu.make_async_copy(own_ref, own_ref, own_send.at[i]).wait)
+
+    @pl.when(row == tp)
+    def _():
+        @pl.loop(1, N_TP)
+        def _(j):
+            pltpu.make_async_copy(places, places, place_send.at[j]).wait()
 
     def left(copies):
         for needed, copy in copies:
@@ -348,9 +418,9 @@
 
     for p in range(len(PARTS)):
         for j in range(REACH // 2 // COLS + 1):
-            if j < REACH // 2 // COLS:
-                left([down(j, p)])
-            left([along(j, s, p) for s in steps(j)])
+            left(down(j, p))
+            left([along(j, s, p) for s in sideways(j)])
+            left(below(j, p))
 
         @pl.loop(0, REACH // 2 + 1)
         def _(k):
@@ -359,20 +429,21 @@
             pl.when(passed)(lambda: pltpu.make_async_copy(gone, gone, across_send.at[k, p]).wait())
 
     for g in range(PER // GROUP):
-        sent = packed.at[g, pl.ds(0, (N_DC - 1) * TILE), :]
+        sent = landed.at[g, pl.ds(0, CHIPS - 1)]
         pltpu.make_async_copy(sent, sent, out_send.at[g]).wait()
+        hand(g).wait_send()
+        written(g).wait()
 
 
 def per_device(queries, keys, values, document_index, owner):
     hbm = pl.BlockSpec(memory_space=pltpu.HBM)
-    vmem = pl.BlockSpec(memory_space=pltpu.VMEM)
     dma = pltpu.SemaphoreType.DMA
     groups, parts = PER // GROUP, len(PARTS)
     return pl.pallas_call(
         kernel,
         out_shape=jax.ShapeDtypeStruct((ROWS, PER * HEAD_DIM), BF16),
         in_specs=[hbm] * 5,
-        out_specs=vmem,
+        out_specs=hbm,
         scratch_shapes=[
             pltpu.VMEM((ROWS, HEAD_DIM), BF16),
             pltpu.VMEM((ROWS, PER * HEAD_DIM), BF16),
@@ -385,13 +456,16 @@
             pltpu.VMEM((N_DC * TILE, GROUP * ROWS), BF16),
             pltpu.VMEM((GROUP * ROWS, N_DC * TILE), BF16),
             pltpu.VMEM((groups, N_DC * TILE, HEAD_DIM), BF16),
-            pltpu.VMEM((groups, N_DC * TILE, HEAD_DIM), BF16),
-            pltpu.VMEM((N_DC, 1, ROWS), I32),
+            pltpu.VMEM((groups, CHIPS, 2 * TILE, HEAD_DIM), BF16),
+            pltpu.VMEM((groups, CHIPS, TILE, HEAD_DIM), BF16),
+            pltpu.VMEM((ROWS, PER * HEAD_DIM), BF16),
+            pltpu.VMEM((2, CHIPS, 1, ROWS), I32),
+            pltpu.VMEM((1, N_DC * TILE), I32),
             pltpu.VMEM((1, ROWS), I32),
             pltpu.VMEM((1, ROWS), I32),
-            dma((2,)), dma((2,)), dma, dma, dma, dma, dma((2,)),
-            dma((4, parts)), dma((5, 7, parts)), dma((REACH // 2 + 1, parts)), dma((SLOTS, parts)), dma((groups,)), dma((groups,)),
-            pltpu.SemaphoreType.REGULAR((4,)),
+            dma((2,)), dma((2,)), dma, dma, dma((COLS + 1,)), dma((2,)), dma((N_TP,)), dma, dma((2,)),
+            dma((4, parts)), dma((4, parts)), dma((5, 7, parts)), dma((REACH // 2 + 1, parts)), dma((SLOTS, parts)), dma((groups,)), dma((groups,)),
+            dma((groups,)), dma((groups,)), dma((groups,)), pltpu.SemaphoreType.REGULAR((3,)),
         ],
         compiler_params=pltpu.CompilerParams(
             collective_id=0, has_side_effects=True, vmem_limit_bytes=63 * 1024 * 1024

time: 63.8 us -> 62.5 us (0.980)
  Pallas kernels: 62 us -> 60.7 us
    pallas_call x1, Pallas kernels: 62 us -> 60.7 us  [per_device(): pl.pallas_call(kernel, out_shape=jax.ShapeDtypeStruct((ROWS, PER * HEAD_D...]
where the time goes in v4:
time: 62.5 us; the launch traced here: 62.4 us
  Pallas kernels  60.7 us (97%)
  local copies, waits for them, and re-layouts  1.67 us (3%)
    pallas_call x1, Pallas kernels, per_device(): pl.pallas_call(kernel, out_shape=jax.ShapeDtypeStruct((ROWS, PER * HEAD_D...  60.7 us
    unnamed x1, local copies, waits for them, and re-layouts  1.67 us

profile of v4, /device:TPU:1, one launch (start us, length us, event | category | flops | bytes accessed | tf_op | source)
XLA Modules:
  0.0 62.4 jit_solution(17795763720906624220)
XLA Ops:
  0.0 60.7 %shard_map.55 = bf16[128,1024]{1,0:T(8,128)(2,1)} custom-call(bf16[16,8192]{1,0:T(8,128)(2,1)} %q_hbm.1, bf16[16,1024]{1,0:T(8,128)(2,1)} %k_hbm.1, bf16[16,1024]{1,0:T(8,128)(2,1)} %v_hbm.1, s32[1,128]{1,0:T(1,128)} %bitcast.2, s32[1,128]{1,0:T(1,128)} %bitcast.3), custom_call_target="tpu_custom_call" | custom-call | flops 2300000000 | bytes 4000000 | tf_op jit(solution)/shard_map/pallas_call | solution.py:442
  60.7 1.7 %copy.7 = bf16[128,1024]{1,0:T(8,128)(2,1)} copy(bf16[128,1024]{1,0:T(8,128)(2,1)} %shard_map.55) | data formatting | bytes 524288

commit v5 on v4

--- a/solution.py
+++ b/solution.py
@@ -39,8 +39,8 @@
 
 def kernel(
     q_hbm, k_hbm, v_hbm, doc_hbm, own_hbm, out_ref,
-    kin, qin, slots, neg, queries, peak, totals, weighted, pack, unpack, packed, landed, handed, attended, owners, places, doc_ref, own_ref,
-    kv_send, kv_recv, q_send, q_recv, own_send, own_recv, place_send, place_recv, doc_sem, down_send, below_send, along_send, across_send, spread_recv, out_send, out_recv, hand_send, hand_recv, out_sem, heard,
+    kin, qin, slots, neg, queries, peak, totals, weighted, pack, unpack, packed, landed, handed, owners, places, doc_ref, own_ref,
+    kv_send, kv_recv, q_send, q_recv, own_send, own_recv, place_send, place_recv, doc_sem, down_send, below_send, along_send, across_send, spread_recv, out_send, out_recv, hand_send, hand_recv, heard,
 ):
     me = lax.axis_index("dc")
     tp = lax.axis_index("tp")
@@ -322,24 +322,24 @@
     from_column(2)
     from_row(1)
     hear(2)
-    send_owner()
     from_column(3)
+    from_row(2)
     pltpu.make_async_copy(qin, qin, q_recv).wait()
     for h in range(PER):
         queries[h * ROWS : (h + 1) * ROWS, :HEAD_DIM] = qin[:, h * HEAD_DIM : (h + 1) * HEAD_DIM]
         queries[h * ROWS : (h + 1) * ROWS, HEAD_DIM:] = neg[...]
+    from_column(4)
+    from_row(3)
+    send_owner()
     step_of(0, (0,))
-    from_row(2)
     step_of(0, (1,))
-    from_column(4)
+    from_row(4)
+    pl.when(row == tp)(gather_owners)
     step_of(1, (0,))
-    from_row(3)
-    pl.when(row == tp)(gather_owners)
     step_of(1, (1,))
+    pl.when(row == tp)(send_places)
     step_of(2, (0,))
     step_of(2, (1,))
-    pl.when(row == tp)(send_places)
-    from_row(4)
 
     for g in every:
         step_of(3, (g,))
@@ -379,10 +379,6 @@
             src_ref=landed.at[g, :, its, :], dst_ref=handed.at[g], send_sem=hand_send.at[g], recv_sem=hand_recv.at[g],
             device_id=(sibling, tp), device_id_type=MESH,
         )
-
-    def written(g):
-        part_of = pl.ds(g * GROUP * HEAD_DIM, GROUP * HEAD_DIM)
-        return pltpu.make_async_copy(attended.at[:, part_of], out_ref.at[:, part_of], out_sem.at[g])
 
     ours = pl.ds(pl.multiple_of(core * TILE, TILE), TILE)
     for g in every:
@@ -395,8 +391,7 @@
         rows = rows.astype(BF16)
         for i in range(GROUP):
             h = g * GROUP + i
-            attended[:, h * HEAD_DIM : (h + 1) * HEAD_DIM] = rows[i * ROWS : (i + 1) * ROWS]
-        written(g).start()
+            out_ref[:, h * HEAD_DIM : (h + 1) * HEAD_DIM] = rows[i * ROWS : (i + 1) * ROWS]
 
     seven = kin.at[pl.ds(0, ROWS - 16), :]
     pltpu.make_async_copy(seven, seven, kv_send.at[0]).wait()
@@ -432,18 +427,18 @@
         sent = landed.at[g, pl.ds(0, CHIPS - 1)]
         pltpu.make_async_copy(sent, sent, out_send.at[g]).wait()
         hand(g).wait_send()
-        written(g).wait()
 
 
 def per_device(queries, keys, values, document_index, owner):
     hbm = pl.BlockSpec(memory_space=pltpu.HBM)
     dma = pltpu.SemaphoreType.DMA
+    operands = (queries, keys, values, document_index.reshape(1, ROWS), owner.reshape(1, ROWS))
     groups, parts = PER // GROUP, len(PARTS)
     return pl.pallas_call(
         kernel,
         out_shape=jax.ShapeDtypeStruct((ROWS, PER * HEAD_DIM), BF16),
         in_specs=[hbm] * 5,
-        out_specs=hbm,
+        out_specs=pl.BlockSpec(memory_space=pltpu.VMEM),
         scratch_shapes=[
             pltpu.VMEM((ROWS, HEAD_DIM), BF16),
             pltpu.VMEM((ROWS, PER * HEAD_DIM), BF16),
@@ -458,20 +453,19 @@
             pltpu.VMEM((groups, N_DC * TILE, HEAD_DIM), BF16),
             pltpu.VMEM((groups, CHIPS, 2 * TILE, HEAD_DIM), BF16),
             pltpu.VMEM((groups, CHIPS, TILE, HEAD_DIM), BF16),
-            pltpu.VMEM((ROWS, PER * HEAD_DIM), BF16),
             pltpu.VMEM((2, CHIPS, 1, ROWS), I32),
             pltpu.VMEM((1, N_DC * TILE), I32),
             pltpu.VMEM((1, ROWS), I32),
             pltpu.VMEM((1, ROWS), I32),
             dma((2,)), dma((2,)), dma, dma, dma((COLS + 1,)), dma((2,)), dma((N_TP,)), dma, dma((2,)),
             dma((4, parts)), dma((4, parts)), dma((5, 7, parts)), dma((REACH // 2 + 1, parts)), dma((SLOTS, parts)), dma((groups,)), dma((groups,)),
-            dma((groups,)), dma((groups,)), dma((groups,)), pltpu.SemaphoreType.REGULAR((3,)),
+            dma((groups,)), dma((groups,)), pltpu.SemaphoreType.REGULAR((3,)),
         ],
         compiler_params=pltpu.CompilerParams(
-            collective_id=0, has_side_effects=True, vmem_limit_bytes=63 * 1024 * 1024
+            collective_id=0, has_side_effects=True, vmem_limit_bytes=48 * 1024 * 1024
         ),
         cost_estimate=pl.CostEstimate(flops=2_300_000_000, bytes_accessed=4_000_000, transcendentals=4_500_000),
-    )(queries, keys, values, document_index.reshape(1, ROWS), owner.reshape(1, ROWS))
+    )(*(pltpu.with_memory_space_constraint(x, pltpu.HBM) for x in operands))
 
 
 def solution(mesh):

time: 62.5 us -> 60.5 us (0.968)
  Pallas kernels: 60.7 us -> 59.7 us
  local copies, waits for them, and re-layouts: 1.67 us -> 0.71 us
    unnamed x1, local copies, waits for them, and re-layouts: 1.67 us -> 0.71 us
    pallas_call x1, Pallas kernels: 60.7 us -> 59.7 us  [per_device(): pl.pallas_call(kernel, out_shape=jax.ShapeDtypeStruct((ROWS, PER * HEAD_D...]
where the time goes in v5:
time: 60.5 us; the launch traced here: 60.4 us
  Pallas kernels  59.7 us (99%)
  local copies, waits for them, and re-layouts  0.71 us (1%)
    pallas_call x1, Pallas kernels, per_device(): pl.pallas_call(kernel, out_shape=jax.ShapeDtypeStruct((ROWS, PER * HEAD_D...  59.7 us

profile of v5, /device:TPU:1, one launch (start us, length us, event | category | flops | bytes accessed | tf_op | source)
XLA Modules:
  0.0 60.4 jit_solution(8399492001196432473)
XLA Ops:
  0.0 59.7 %shard_map.55 = bf16[128,1024]{1,0:T(8,128)(2,1)S(1)} custom-call(bf16[16,8192]{1,0:T(8,128)(2,1)} %q_hbm.1, bf16[16,1024]{1,0:T(8,128)(2,1)} %k_hbm.1, bf16[16,1024]{1,0:T(8,128)(2,1)} %v_hbm.1, s32[1,128]{1,0:T(1,128)} %bitcast.2, s32[1,128]{1,0:T(1,128)} %bitcast.3), custom_call_target="tpu_custom_call" | custom-call | flops 2300000000 | bytes 4000000 | tf_op jit(solution)/shard_map/pallas_call | solution.py:437
  59.7 0.7 %copy.7 = bf16[128,1024]{1,0:T(8,128)(2,1)} copy(bf16[128,1024]{1,0:T(8,128)(2,1)S(1)} %shard_map.55) | data formatting | bytes 524288

commit v6 on v5

--- a/solution.py
+++ b/solution.py
@@ -39,12 +39,18 @@
 
 def kernel(
     q_hbm, k_hbm, v_hbm, doc_hbm, own_hbm, out_ref,
-    kin, qin, slots, neg, queries, peak, totals, weighted, pack, unpack, packed, landed, handed, owners, places, doc_ref, own_ref,
-    kv_send, kv_recv, q_send, q_recv, own_send, own_recv, place_send, place_recv, doc_sem, down_send, below_send, along_send, across_send, spread_recv, out_send, out_recv, hand_send, hand_recv, heard,
+    k_near, v_near, kin, qin, slots, neg, queries, peak, totals, weighted, pack, unpack, packed, landed, handed, owners, places, doc_ref, own_ref,
+    stage_sem, kv_send, kv_recv, q_send, q_recv, own_send, own_recv, place_send, place_recv, doc_sem, down_send, below_send, along_send, across_send, spread_recv, out_send, out_recv, hand_send, hand_recv, heard,
 ):
     me = lax.axis_index("dc")
     tp = lax.axis_index("tp")
 
+    staged = [
+        pltpu.make_async_copy(k_hbm, k_near, stage_sem.at[0]),
+        pltpu.make_async_copy(v_hbm, v_near, stage_sem.at[1]),
+    ]
+    for copy in staged:
+        copy.start()
     pltpu.make_async_copy(doc_hbm, doc_ref, doc_sem.at[0]).start()
     pltpu.make_async_copy(own_hbm, own_ref, doc_sem.at[1]).start()
     chip, core = me // 2, lax.rem(me, 2)
@@ -93,16 +99,18 @@
             device_id=(me, t), device_id_type=MESH,
         )
 
+    for copy in staged:
+        copy.wait()
     value_target = slots.at[0, pl.ds(pl.multiple_of(V0 + tp * 16, 16), 16), :]
 
     @pl.loop(1, N_TP)
     def _(j):
         t = lax.rem(tp + j, N_TP)
-        part(k_hbm, t, HEAD_DIM, kin.at[mine, :], kv_send.at[0], kv_recv.at[0]).start()
-        part(v_hbm, t, HEAD_DIM, value_target, kv_send.at[1], kv_recv.at[1]).start()
-
-    pltpu.make_async_copy(k_hbm.at[:, columns(tp, HEAD_DIM)], kin.at[mine, :], kv_recv.at[0]).start()
-    pltpu.make_async_copy(v_hbm.at[:, columns(tp, HEAD_DIM)], value_target, kv_recv.at[1]).start()
+        part(k_near, t, HEAD_DIM, kin.at[mine, :], kv_send.at[0], kv_recv.at[0]).start()
+        part(v_near, t, HEAD_DIM, value_target, kv_send.at[1], kv_recv.at[1]).start()
+
+    pltpu.make_async_copy(k_near.at[:, columns(tp, HEAD_DIM)], kin.at[mine, :], kv_recv.at[0]).start()
+    pltpu.make_async_copy(v_near.at[:, columns(tp, HEAD_DIM)], value_target, kv_recv.at[1]).start()
 
     @pl.loop(1, N_TP)
     def _(j):
@@ -440,6 +448,8 @@
         in_specs=[hbm] * 5,
         out_specs=pl.BlockSpec(memory_space=pltpu.VMEM),
         scratch_shapes=[
+            pltpu.VMEM((16, KVH * HEAD_DIM), BF16),
+            pltpu.VMEM((16, KVH * HEAD_DIM), BF16),
             pltpu.VMEM((ROWS, HEAD_DIM), BF16),
             pltpu.VMEM((ROWS, PER * HEAD_DIM), BF16),
             pltpu.VMEM((SLOTS, END, ROWS), BF16),
@@ -457,7 +467,7 @@
             pltpu.VMEM((1, N_DC * TILE), I32),
             pltpu.VMEM((1, ROWS), I32),
             pltpu.VMEM((1, ROWS), I32),
-            dma((2,)), dma((2,)), dma, dma, dma((COLS + 1,)), dma((2,)), dma((N_TP,)), dma, dma((2,)),
+            dma((2,)), dma((2,)), dma((2,)), dma, dma, dma((COLS + 1,)), dma((2,)), dma((N_TP,)), dma, dma((2,)),
             dma((4, parts)), dma((4, parts)), dma((5, 7, parts)), dma((REACH // 2 + 1, parts)), dma((SLOTS, parts)), dma((groups,)), dma((groups,)),
             dma((groups,)), dma((groups,)), pltpu.SemaphoreType.REGULAR((3,)),
         ],

time: 60.5 us -> 60.3 us (level)
  no operation moved by 1% of the time
where the time goes in v6:
time: 60.3 us; the launch traced here: 60.2 us
  Pallas kernels  59.4 us (99%)
  local copies, waits for them, and re-layouts  0.71 us (1%)
    pallas_call x1, Pallas kernels, per_device(): pl.pallas_call(kernel, out_shape=jax.ShapeDtypeStruct((ROWS, PER * HEAD_D...  59.4 us

profile of v6, /device:TPU:1, one launch (start us, length us, event | category | flops | bytes accessed | tf_op | source)
XLA Modules:
  0.0 60.2 jit_solution(13333229767440363489)
XLA Ops:
  0.0 59.4 %shard_map.55 = bf16[128,1024]{1,0:T(8,128)(2,1)S(1)} custom-call(bf16[16,8192]{1,0:T(8,128)(2,1)} %q_hbm.1, bf16[16,1024]{1,0:T(8,128)(2,1)} %k_hbm.1, bf16[16,1024]{1,0:T(8,128)(2,1)} %v_hbm.1, s32[1,128]{1,0:T(1,128)} %bitcast.2, s32[1,128]{1,0:T(1,128)} %bitcast.3), custom_call_target="tpu_custom_call" | custom-call | flops 2300000000 | bytes 4000000 | tf_op jit(solution)/shard_map/pallas_call | solution.py:445
  59.4 0.7 %copy.7 = bf16[128,1024]{1,0:T(8,128)(2,1)} copy(bf16[128,1024]{1,0:T(8,128)(2,1)S(1)} %shard_map.55) | data formatting | bytes 524288
